TPU v7x, 128 devices: a whole 4x4x4 slice. The times are simulated.
128 devices in a mesh: box: 16 (over z, x), dir: 8 (over y, core).
Axes of the slice: x: 4, y: 4, z: 4, core: 2. Of those that a mesh axis runs over, the one named last changes fastest.
Arguments:
- currents: bfloat16 [2, 3072, 128, 256], P(None, ('box', 'dir')), may hold values from -6 to 6
- near_tiles: bfloat16 [3072, 9, 2, 128, 128], P(('box', 'dir')), may hold values from -0.125 to 0.125
- near_index: int32 [3072, 9], P(('box', 'dir')), may hold values from 0 to 3071, as said below
- near_count: int32 [3072], P(('box', 'dir')), may hold values from 2 to 9
- radiate: bfloat16 [3072, 2, 128, 128], P(('box', 'dir')), may hold values from -0.375 to 0.375
- receive: bfloat16 [3072, 2, 128, 128], P(('box', 'dir')), may hold values from -0.375 to 0.375
- interp: bfloat16 [512, 128], replicated, may hold values from -0.1875 to 0.1875
- shift_angle: float32 [8, 512], replicated, may hold values from -3.140625 to 3.140625
- far_index: int32 [384, 48], replicated, may hold values from 0 to 383, as said below
- far_count: int32 [384], replicated, may hold values from 12 to 48
- trans_index: int32 [384, 48], replicated, may hold values from 0 to 315
- translators: float32 [316, 2, 512], P(None, None, ('box', 'dir')), may hold values from -0.625 to 0.625
Outputs:
- response: bfloat16 [2, 3072, 128, 256], P(None, ('box', 'dir'))
Inputs may be any that keep to these rules, and one draw needn't show every extreme that they name: `near_index`: slot 0 of box b is b itself; every entry lies within 12 of its own box's index. `far_index`: no parent box lists itself.
All inputs are finite; a program needn't handle non-finite values.
Results may differ from a plain program's by a relative error of at most 0.007.
Values may be sent and summed in bfloat16 or wider, within the bound.
No kernel may reach another device: no remote copies, remote signals or barrier semaphores. Data moves between devices by JAX's collectives and lax.ppermute only.
A program may use at most 256 MiB of HBM per device.

v0:
```python
import jax
import jax.numpy as jnp
from jax import lax
from jax.experimental import pallas as pl
from jax.experimental.pallas import tpu as pltpu
from jax.sharding import PartitionSpec as P

BF16 = jnp.bfloat16
F32 = jnp.float32
AXES = ("box", "dir")
MIB = 1 << 20
OFF = 1 << 10


def passed_along(value, axis, by):
    peers = lax.axis_size(axis)
    pairs = [(i, i + by) for i in range(peers) if 0 <= i + by < peers]
    return lax.ppermute(value, axis, pairs)


def dot(left, right):
    return jnp.dot(left, right, preferred_element_type=F32)


def embedded(real, imag):
    return jnp.concatenate(
        [jnp.concatenate([real, -imag], axis=1), jnp.concatenate([imag, real], axis=1)], axis=0
    )


def interleave(upper, lower):
    rows, columns = upper.shape
    a = upper.reshape(rows // 8, 8, columns)
    b = lower.reshape(rows // 8, 8, columns)
    first = lax.broadcasted_iota(jnp.int32, a.shape, 1) < 4
    t = jnp.where(first, a, pltpu.roll(b, 4, 1))
    u = jnp.where(first, pltpu.roll(a, 4, 1), b)
    return jnp.stack([t, u], axis=1).reshape(2 * rows, columns)


def separate(mixed):
    rows, columns = mixed.shape
    parts = mixed.reshape(rows // 16, 2, 8, columns)
    t, u = parts[:, 0], parts[:, 1]
    first = lax.broadcasted_iota(jnp.int32, t.shape, 1) < 4
    a = jnp.where(first, t, pltpu.roll(u, 4, 1))
    b = jnp.where(first, pltpu.roll(t, 4, 1), u)
    return jnp.concatenate([a, b], axis=0).reshape(rows, columns)


def upward_kernel(cur_ref, rad_ref, interp_ref, angle_ref, out_ref, w_ref, leaf_ref):
    half = interp_ref.shape[0]

    @pl.when(pl.program_id(0) == 0)
    def _():
        angle = angle_ref[...]
        cosine = jnp.cos(angle).T
        sine = jnp.sin(angle).T
        interp = interp_ref[...].astype(F32)
        for c in range(8):
            ci = (cosine[:, c : c + 1] * interp).astype(BF16)
            si = (sine[:, c : c + 1] * interp).astype(BF16)
            w_ref[:half, c * 256 : c * 256 + 128] = ci
            w_ref[:half, c * 256 + 128 : c * 256 + 256] = -si
            w_ref[half:, c * 256 : c * 256 + 128] = si
            w_ref[half:, c * 256 + 128 : c * 256 + 256] = ci

    for c in range(8):
        x = cur_ref[:, c].reshape(256, 256)
        leaf = dot(embedded(rad_ref[c, 0], rad_ref[c, 1]), x)
        leaf_ref[c * 256 : (c + 1) * 256, :] = leaf.astype(BF16)
    y = dot(w_ref[...], leaf_ref[...])
    out_ref[...] = interleave(y[:half], y[half:]).astype(BF16)


def upward(currents, radiate, interp, angle):
    parents = currents.shape[1] // 8
    directions = interp.shape[0]
    return pl.pallas_call(
        upward_kernel,
        grid=(parents,),
        in_specs=[
            pl.BlockSpec((2, 8, 128, 256), lambda p: (0, p, 0, 0)),
            pl.BlockSpec((8, 2, 128, 128), lambda p: (p, 0, 0, 0)),
            pl.BlockSpec((directions, 128), lambda p: (0, 0)),
            pl.BlockSpec((8, directions), lambda p: (0, 0)),
        ],
        out_specs=pl.BlockSpec((2 * directions, 256), lambda p: (0, p)),
        out_shape=jax.ShapeDtypeStruct((2 * directions, parents * 256), BF16),
        scratch_shapes=[
            pltpu.VMEM((2 * directions, 2048), BF16),
            pltpu.VMEM((2048, 256), BF16),
        ],
        compiler_params=pltpu.CompilerParams(vmem_limit_bytes=60 * MIB),
        cost_estimate=pl.CostEstimate(flops=5_000_000_000, bytes_accessed=7_000_000, transcendentals=0),
        name="upward",
    )(currents, radiate, interp, angle)


def operators_kernel(pair_ref, table_ref, out_ref, mask_ref):
    slots = mask_ref.shape[1] // 16

    @pl.when(pl.program_id(0) == 0)
    def _():
        row = lax.broadcasted_iota(jnp.int32, mask_ref.shape, 0) % 16
        column = lax.broadcasted_iota(jnp.int32, mask_ref.shape, 1) // slots
        mask_ref[...] = jnp.where(row == column, 1.0, 0.0)

    def picks(size, index):
        ids = lax.broadcasted_iota(jnp.int32, (size, index.shape[1]), 0)
        return jnp.where(ids == index, 1.0, 0.0).astype(BF16)

    pair = pair_ref[0]
    factor = dot(table_ref[...], picks(table_ref.shape[1], pair & (OFF - 1)))
    factor = (factor * mask_ref[...]).astype(BF16)
    block = lax.dot_general(
        factor,
        picks(out_ref.shape[2], pair >> 10),
        (((1,), (1,)), ((), ())),
        preferred_element_type=F32,
    )
    out_ref[...] = block.reshape(out_ref.shape).astype(BF16)


def operators(pairs, table):
    blocks, _, width = pairs.shape
    parents = blocks * 16
    return pl.pallas_call(
        operators_kernel,
        grid=(blocks,),
        in_specs=[
            pl.BlockSpec((1, 1, width), lambda i: (i, 0, 0)),
            pl.BlockSpec(table.shape, lambda i: (0, 0)),
        ],
        out_specs=pl.BlockSpec((8, 16, parents), lambda i: (0, i, 0)),
        out_shape=jax.ShapeDtypeStruct((8, parents, parents), BF16),
        scratch_shapes=[pltpu.VMEM((128, width), F32)],
        compiler_params=pltpu.CompilerParams(vmem_limit_bytes=60 * MIB),
        cost_estimate=pl.CostEstimate(flops=12_000_000_000, bytes_accessed=3_000_000, transcendentals=0),
        name="operators",
    )(pairs, table)


def translate_kernel(x_ref, m_ref, out_ref, xs_ref, xj_ref, ys_ref):
    devices = x_ref.shape[0] // 8
    tiles = x_ref.shape[1] // 128
    for t in range(tiles):
        xs_ref[t] = x_ref[:, t * 128 : (t + 1) * 128].astype(F32)
    for j in range(4):
        for c in range(2):
            for t in range(tiles):
                rows = (c * (tiles // 2) + t // 2) * devices
                lanes = (t % 2) * 128
                xj_ref[rows : rows + devices, lanes : lanes + 128] = xs_ref[
                    t, pl.ds(c * 4 + j, devices, stride=8), :
                ].astype(BF16)
        real, imag = m_ref[2 * j], m_ref[2 * j + 1]
        x = xj_ref[...]
        for c, row in enumerate(((real, -imag), (imag, real))):
            y = dot(jnp.concatenate(row, axis=1), x)
            for t in range(tiles):
                ys_ref[t, pl.ds(c * 4 + j, devices, stride=8), :] = y[
                    (t // 2) * devices : (t // 2 + 1) * devices, (t % 2) * 128 : (t % 2) * 128 + 128
                ]
    for t in range(tiles):
        out_ref[:, t * 128 : (t + 1) * 128] = ys_ref[t].astype(BF16)


def translate(x, matrix):
    rows, width = x.shape
    tiles = width // 128
    return pl.pallas_call(
        translate_kernel,
        in_specs=[pl.BlockSpec(memory_space=pltpu.VMEM)] * 2,
        out_specs=pl.BlockSpec(memory_space=pltpu.VMEM),
        out_shape=jax.ShapeDtypeStruct(x.shape, BF16),
        scratch_shapes=[
            pltpu.VMEM((tiles, rows, 128), F32),
            pltpu.VMEM((rows // 8 * tiles, 256), BF16),
            pltpu.VMEM((tiles, rows, 128), F32),
        ],
        compiler_params=pltpu.CompilerParams(vmem_limit_bytes=60 * MIB),
        cost_estimate=pl.CostEstimate(flops=1_200_000_000, bytes_accessed=5_500_000, transcendentals=0),
        name="translate",
    )(x, matrix)


def near_kernel(index_ref, count_ref, low_ref, cur_ref, up_ref, tile_ref, out_ref, win_ref, sems):
    step = pl.program_id(0)
    group, slots = tile_ref.shape[:2]
    reach = low_ref.shape[1]
    boxes = cur_ref.shape[1]

    @pl.when(step == 0)
    def _():
        copies = []
        for c in range(2):
            rows = pl.ds(c * 128, 128)
            starts = ((low_ref, 0, reach), (cur_ref, reach, boxes), (up_ref, reach + boxes, reach))
            for n, (source, start, size) in enumerate(starts):
                copies.append(
                    pltpu.make_async_copy(
                        source.at[c], win_ref.at[pl.ds(start, size), rows, :], sems.at[c * 3 + n]
                    )
                )
        for copy in copies:
            copy.start()
        for copy in copies:
            copy.wait()

    @pl.loop(0, group)
    def _(i):
        box = step * group + i
        for live in range(1, slots + 1):

            @pl.when(count_ref[box] == live)
            def _():
                tiles = [embedded(tile_ref[i, s, 0], tile_ref[i, s, 1]) for s in range(live)]
                picked = [win_ref[index_ref[box * slots + s]] for s in range(live)]
                out_ref[i] = dot(
                    jnp.concatenate(tiles, axis=1), jnp.concatenate(picked, axis=0)
                ).astype(out_ref.dtype)


def near(index, count, low, currents, up, tiles):
    boxes, slots = tiles.shape[:2]
    reach = low.shape[1]
    group = 4
    return pl.pallas_call(
        near_kernel,
        grid_spec=pltpu.PrefetchScalarGridSpec(
            num_scalar_prefetch=2,
            grid=(boxes // group,),
            in_specs=[
                pl.BlockSpec(memory_space=pl.ANY),
                pl.BlockSpec(memory_space=pl.ANY),
                pl.BlockSpec(memory_space=pl.ANY),
                pl.BlockSpec((group, slots, 2, 128, 128), lambda b, i, n: (b, 0, 0, 0, 0)),
            ],
            out_specs=pl.BlockSpec((group, 256, 256), lambda b, i, n: (b, 0, 0)),
            scratch_shapes=[
                pltpu.VMEM((boxes + 2 * reach, 256, 256), BF16),
                pltpu.SemaphoreType.DMA((6,)),
            ],
        ),
        out_shape=jax.ShapeDtypeStruct((boxes, 256, 256), BF16),
        compiler_params=pltpu.CompilerParams(vmem_limit_bytes=60 * MIB),
        cost_estimate=pl.CostEstimate(flops=7_200_000_000, bytes_accessed=27_000_000, transcendentals=0),
        name="near",
    )(index, count, low, currents, up, tiles)


def downward_kernel(z_ref, rec_ref, interp_ref, angle_ref, near_ref, out_ref, w_ref, arr_ref):
    half = angle_ref.shape[1]

    @pl.when(pl.program_id(0) == 0)
    def _():
        angle = angle_ref[...]
        cosine = jnp.cos(angle)
        sine = jnp.sin(angle)
        interp = interp_ref[...].astype(F32).T
        for c in range(8):
            ci = (cosine[c : c + 1] * interp).astype(BF16)
            si = (sine[c : c + 1] * interp).astype(BF16)
            w_ref[c * 256 : c * 256 + 128, :half] = ci
            w_ref[c * 256 : c * 256 + 128, half:] = si
            w_ref[c * 256 + 128 : c * 256 + 256, :half] = -si
            w_ref[c * 256 + 128 : c * 256 + 256, half:] = ci

    z = separate(z_ref[...].astype(F32)).astype(BF16)
    arr_ref[...] = dot(w_ref[...], z).astype(BF16)
    for c in range(8):
        far = dot(embedded(rec_ref[c, 0], rec_ref[c, 1]), arr_ref[c * 256 : (c + 1) * 256, :])
        out_ref[:, c] = (far + near_ref[c].astype(F32)).astype(BF16).reshape(2, 128, 256)


def downward(z, receive, interp, angle, near_field):
    boxes = receive.shape[0]
    directions = interp.shape[0]
    return pl.pallas_call(
        downward_kernel,
        grid=(boxes // 8,),
        in_specs=[
            pl.BlockSpec((2 * directions, 256), lambda p: (0, p)),
            pl.BlockSpec((8, 2, 128, 128), lambda p: (p, 0, 0, 0)),
            pl.BlockSpec((directions, 128), lambda p: (0, 0)),
            pl.BlockSpec((8, directions), lambda p: (0, 0)),
            pl.BlockSpec((8, 256, 256), lambda p: (p, 0, 0)),
        ],
        out_specs=pl.BlockSpec((2, 8, 128, 256), lambda p: (0, p, 0, 0)),
        out_shape=jax.ShapeDtypeStruct((2, boxes, 128, 256), BF16),
        scratch_shapes=[
            pltpu.VMEM((2048, 2 * directions), BF16),
            pltpu.VMEM((2048, 256), BF16),
        ],
        compiler_params=pltpu.CompilerParams(vmem_limit_bytes=60 * MIB),
        cost_estimate=pl.CostEstimate(flops=5_000_000_000, bytes_accessed=13_000_000, transcendentals=0),
        name="downward",
    )(z, receive, interp, angle, near_field)


def exchanged(value):
    return lax.all_to_all(value, AXES, split_axis=0, concat_axis=0, tiled=True)


def local(
    currents,
    near_tiles,
    near_index,
    near_count,
    radiate,
    receive,
    interp,
    shift_angle,
    far_index,
    far_count,
    trans_index,
    translators,
):
    boxes = currents.shape[1]
    reach = boxes // 2
    owned = boxes // 8
    parents, slots = far_index.shape
    devices = parents // owned
    lower = passed_along(currents[:, boxes - reach :], AXES, 1)
    upper = passed_along(currents[:, :reach], AXES, -1)

    sent = upward(currents, radiate, interp, shift_angle)
    by_direction = exchanged(sent)

    def blocks(value):
        value = value.reshape(devices, owned, slots).transpose(1, 0, 2)
        return value.reshape(parents // 16, 1, 16 * slots)

    live = jnp.arange(slots, dtype=jnp.int32)[None, :] < far_count[:, None]
    source = jnp.where(live, far_index % owned * devices + far_index // owned, OFF)
    pairs = blocks(source * OFF + trans_index)
    table = translators.transpose(2, 1, 0).reshape(8, -1).astype(BF16)
    table = jnp.pad(table, ((0, 0), (0, -table.shape[1] % 128)))
    table = jnp.repeat(table, 16, axis=0)
    matrix = operators(pairs, table)

    back = translate(by_direction, matrix)
    incoming = exchanged(back)

    first = lax.axis_index(AXES) * boxes - reach
    near_field = near(
        (near_index - first).reshape(-1), near_count, lower, currents, upper, near_tiles
    )
    return downward(incoming, receive, interp, shift_angle, near_field)


def solution(mesh):
    placed = (
        P(None, AXES, None, None),
        P(AXES, None, None, None, None),
        P(AXES, None),
        P(AXES),
        P(AXES, None, None, None),
        P(AXES, None, None, None),
        P(),
        P(),
        P(),
        P(),
        P(),
        P(None, None, AXES),
    )
    return jax.shard_map(
        local,
        mesh=mesh,
        in_specs=placed,
        out_specs=P(None, AXES, None, None),
        check_vma=False,
    )
```

profile of v0, /device:TPU:1, one launch (start us, length us, event | category | flops | bytes accessed | tf_op | source)
XLA Modules:
  0.0 104.6 jit_solution(17482865582359360603)
XLA Ops:
  0.0 8.4 %upward.1 = bf16[1024,768]{1,0:T(8,128)(2,1)} custom-call(bf16[2,24,128,256]{3,2,1,0:T(8,128)(2,1)} %cur_ref.3, bf16[24,2,128,128]{3,2,1,0:T(8,128)(2,1)} %rad_ref.1, bf16[512,128]{1,0:T(8,128)(2,1)} %interp_ref.3, f32[8,512]{1,0:T(8,128)} %angle_ref.3), custom_call_target="tpu_custom_call" | custom-call | flops 5000000000 | bytes 7000000 | tf_op jit(solution)/shard_map/upward/pallas_call | solution.py:79
  8.4 11.5 %all-to-all-start = ((bf16[128,8,768]{2,1,0:T(8,128)(2,1)}), bf16[128,8,768]{2,1,0:T(8,128)(2,1)S(1)}, u32[]{:S(2)}, u32[]{:S(2)}) async-start(bf16[128,8,768]{2,1,0:T(8,128)(2,1)} %bitcast.11), calls=%async_computation | async-start | bytes 3145728 | tf_op jit(solution)/shard_map/all_to_all | solution.py:303
  19.9 0.0 copy-start.4
  19.9 0.0 copy-start.2
  19.9 0.0 copy-start.3
  19.9 0.0 copy-start.6
  19.9 3.5 %fusion.6 = (bf16[2,12,128,256]{3,2,1,0:T(8,128)(2,1)}, bf16[2,12,128,256]{3,2,1,0:T(8,128)(2,1)S(1)}) fusion(bf16[2,24,128,256]{3,2,1,0:T(8,128)(2,1)} %cur_ref.3), kind=kLoop, calls=%fused_computation.13 | loop fusion | bytes 6291456 | tf_op jit(solution)/shard_map/slice | solution.py:326
  23.4 3.0 %collective-permute-start.1 = (bf16[2,12,128,256]{3,2,1,0:T(8,128)(2,1)}, bf16[2,12,128,256]{3,2,1,0:T(8,128)(2,1)}, u32[]{:S(2)}, u32[]{:S(2)}) collective-permute-start(bf16[2,12,128,256]{3,2,1,0:T(8,128)(2,1)} %get-tuple-element.5), channel_id=1, source_target_pairs={{1,0},{2,1},{3,2},{4,3},{5,4},{6,5},{7,6},{8,7},{9,8},{10,9},{11,1... | collective-permute-start | bytes 4718600 | tf_op jit(solution)/shard_map/ppermute | solution.py:18
  26.4 2.6 %collective-permute-start = (bf16[2,12,128,256]{3,2,1,0:T(8,128)(2,1)S(1)}, bf16[2,12,128,256]{3,2,1,0:T(8,128)(2,1)}, u32[]{:S(2)}, u32[]{:S(2)}) collective-permute-start(bf16[2,12,128,256]{3,2,1,0:T(8,128)(2,1)S(1)} %get-tuple-element.6), channel_id=1, source_target_pairs={{0,1},{1,2},{2,3},{3,4},{4,5},{5,6},{6,7},{7,8},{8,9},{9,10},{10,1... | collective-permute-start | bytes 4718600 | tf_op jit(solution)/shard_map/ppermute | solution.py:18
  29.0 0.0 copy-done.4
  29.0 0.0 copy-done.2
  29.0 0.0 copy-done.3
  29.0 0.0 copy-done.6
  29.0 0.1 fusion.4
  29.1 0.8 copy.14
  30.0 1.0 reshape.19
  31.0 0.7 copy.15
  31.7 1.7 %reshape.23.pair_ref = s32[24,1,768]{2,1,0:T(1,128)} reshape(s32[3,128,48]{2,1,0:T(8,128)} %copy.15) | data formatting | bytes 147456 | tf_op jit(solution)/shard_map/reshape | solution.py:333
  33.4 0.6 broadcast_in_dim.10
  34.1 16.0 %operators.1.m_ref = bf16[8,384,384]{2,1,0:T(8,128)(2,1)} custom-call(s32[24,1,768]{2,1,0:T(1,128)} %reshape.23.pair_ref, bf16[128,384]{1,0:T(8,128)(2,1)} %bitcast.13), custom_call_target="tpu_custom_call" | custom-call | flops 12000000000 | bytes 3000000 | tf_op jit(solution)/shard_map/operators/pallas_call | solution.py:128
  50.1 0.0 all-to-all-done
  50.1 1.1 %copy-done = bf16[128,8,768]{2,1,0:T(8,128)(2,1)} copy-done((bf16[128,8,768]{2,1,0:T(8,128)(2,1)}, bf16[128,8,768]{2,1,0:T(8,128)(2,1)S(1)}, u32[]{:S(2)}) %copy-start) | copy-done | bytes 1572888
  51.2 5.5 %translate.1 = bf16[1024,768]{1,0:T(8,128)(2,1)} custom-call(bf16[1024,768]{1,0:T(8,128)(2,1)} %bitcast.9, bf16[8,384,384]{2,1,0:T(8,128)(2,1)} %operators.1.m_ref), custom_call_target="tpu_custom_call" | custom-call | flops 1200000000 | bytes 5500000 | tf_op jit(solution)/shard_map/translate/pallas_call | solution.py:172
  56.8 13.2 %all-to-all-start.1 = ((bf16[128,8,768]{2,1,0:T(8,128)(2,1)}), bf16[128,8,768]{2,1,0:T(8,128)(2,1)S(1)}, u32[]{:S(2)}, u32[]{:S(2)}) async-start(bf16[128,8,768]{2,1,0:T(8,128)(2,1)} %bitcast.8), calls=%async_computation.1 | async-start | bytes 3145728 | tf_op jit(solution)/shard_map/all_to_all | solution.py:303
  70.0 0.1 copy.18
  70.1 0.7 reshape.22.index_ref
  70.8 0.0 collective-permute-done.1.up_ref
  70.8 0.0 collective-permute-done.low_ref
  70.8 16.5 %near.1.near_ref = bf16[24,256,256]{2,1,0:T(8,128)(2,1)} custom-call(s32[216]{0:T(256)} %reshape.22.index_ref, s32[24]{0:T(128)} %count_ref.1, bf16[2,12,128,256]{3,2,1,0:T(8,128)(2,1)} %collective-permute-done.low_ref, bf16[2,24,128,256]{3,2,1,0:T(8,128)(2,1)} %cur_ref.3, bf16[2,12,128,256]{3,2,1,0:T(8,128)(2,1)} %collective-permute-done.1.up_ref, ...), custom_call_target="tpu_custom_call" | custom-call | flops 7200000000 | bytes 27000000 | tf_op jit(solution)/shard_map/near/pallas_call | solution.py:229
  87.3 7.2 %all-to-all-done.1 = bf16[128,8,768]{2,1,0:T(8,128)(2,1)S(1)} async-done(((bf16[128,8,768]{2,1,0:T(8,128)(2,1)}), bf16[128,8,768]{2,1,0:T(8,128)(2,1)S(1)}, u32[]{:S(2)}, u32[]{:S(2)}) %all-to-all-start.1) | async-done | bytes 1572896 | tf_op jit(solution)/shard_map/all_to_all | solution.py:303
  94.6 1.2 %copy-done.1 = bf16[128,8,768]{2,1,0:T(8,128)(2,1)} copy-done((bf16[128,8,768]{2,1,0:T(8,128)(2,1)}, bf16[128,8,768]{2,1,0:T(8,128)(2,1)S(1)}, u32[]{:S(2)}) %copy-start.1) | copy-done | bytes 1572888
  95.7 8.8 %downward.1 = bf16[2,24,128,256]{3,2,1,0:T(8,128)(2,1)} custom-call(bf16[1024,768]{1,0:T(8,128)(2,1)} %bitcast.10, bf16[24,2,128,128]{3,2,1,0:T(8,128)(2,1)} %rec_ref.1, bf16[512,128]{1,0:T(8,128)(2,1)} %interp_ref.3, f32[8,512]{1,0:T(8,128)} %angle_ref.3, bf16[24,256,256]{2,1,0:T(8,128)(2,1)} %near.1.near_ref), custom_call_target="tpu_custom_call" | custom-call | flops 5000000000 | bytes 13000000 | tf_op jit(solution)/shard_map/downward/pallas_call | solution.py:280
  (9 shorter events, 0.0 us)
Async XLA Ops:
  8.4 41.7 %all-to-all-start = ((bf16[128,8,768]{2,1,0:T(8,128)(2,1)}), bf16[128,8,768]{2,1,0:T(8,128)(2,1)S(1)}, u32[]{:S(2)}, u32[]{:S(2)}) async-start(bf16[128,8,768]{2,1,0:T(8,128)(2,1)} %bitcast.11), calls=%async_computation | async-start | bytes 3145728 | tf_op jit(solution)/shard_map/all_to_all | solution.py:303
  19.9 9.1 %copy-start.4 = (f32[316,2,4]{0,2,1:T(4,128)S(1)}, f32[316,2,4]{0,2,1:T(4,128)}, u32[]{:S(2)}) copy-start(f32[316,2,4]{0,2,1:T(4,128)} %param.23) | copy-start | bytes 30340
  19.9 9.1 %copy-start.2 = (s32[384,48]{0,1:T(8,128)S(1)}, s32[384,48]{0,1:T(8,128)}, u32[]{:S(2)}) copy-start(s32[384,48]{0,1:T(8,128)} %param.22) | copy-start | bytes 221188
  19.9 9.1 %copy-start.3 = (s32[384,48]{0,1:T(8,128)S(1)}, s32[384,48]{0,1:T(8,128)}, u32[]{:S(2)}) copy-start(s32[384,48]{0,1:T(8,128)} %param.20) | copy-start | bytes 221188
  19.9 9.1 %copy-start.6 = (s32[384]{0:T(512)S(1)}, s32[384]{0:T(512)}, u32[]{:S(2)}) copy-start(s32[384]{0:T(512)} %param.21) | copy-start | bytes 4612
  23.4 47.4 %collective-permute-start.1 = (bf16[2,12,128,256]{3,2,1,0:T(8,128)(2,1)}, bf16[2,12,128,256]{3,2,1,0:T(8,128)(2,1)}, u32[]{:S(2)}, u32[]{:S(2)}) collective-permute-start(bf16[2,12,128,256]{3,2,1,0:T(8,128)(2,1)} %get-tuple-element.5), channel_id=1, source_target_pairs={{1,0},{2,1},{3,2},{4,3},{5,4},{6,5},{7,6},{8,7},{9,8},{10,9},{11,1... | collective-permute-start | bytes 4718600 | tf_op jit(solution)/shard_map/ppermute | solution.py:18
  26.4 44.4 %collective-permute-start = (bf16[2,12,128,256]{3,2,1,0:T(8,128)(2,1)S(1)}, bf16[2,12,128,256]{3,2,1,0:T(8,128)(2,1)}, u32[]{:S(2)}, u32[]{:S(2)}) collective-permute-start(bf16[2,12,128,256]{3,2,1,0:T(8,128)(2,1)S(1)} %get-tuple-element.6), channel_id=1, source_target_pairs={{0,1},{1,2},{2,3},{3,4},{4,5},{5,6},{6,7},{7,8},{8,9},{9,10},{10,1... | collective-permute-start | bytes 4718600 | tf_op jit(solution)/shard_map/ppermute | solution.py:18
  50.1 1.1 %copy-start = (bf16[128,8,768]{2,1,0:T(8,128)(2,1)}, bf16[128,8,768]{2,1,0:T(8,128)(2,1)S(1)}, u32[]{:S(2)}) copy-start(bf16[128,8,768]{2,1,0:T(8,128)(2,1)S(1)} %all-to-all-done) | copy-start | bytes 4718596
  56.8 13.3 %copy-start.5 = (s32[24,9]{0,1:T(8,128)S(1)}, s32[24,9]{0,1:T(8,128)}, u32[]{:S(2)}) copy-start(s32[24,9]{0,1:T(8,128)} %param.14) | copy-start | bytes 2596
  56.8 37.8 %all-to-all-start.1 = ((bf16[128,8,768]{2,1,0:T(8,128)(2,1)}), bf16[128,8,768]{2,1,0:T(8,128)(2,1)S(1)}, u32[]{:S(2)}, u32[]{:S(2)}) async-start(bf16[128,8,768]{2,1,0:T(8,128)(2,1)} %bitcast.8), calls=%async_computation.1 | async-start | bytes 3145728 | tf_op jit(solution)/shard_map/all_to_all | solution.py:303
  94.6 1.2 %copy-start.1 = (bf16[128,8,768]{2,1,0:T(8,128)(2,1)}, bf16[128,8,768]{2,1,0:T(8,128)(2,1)S(1)}, u32[]{:S(2)}) copy-start(bf16[128,8,768]{2,1,0:T(8,128)(2,1)S(1)} %all-to-all-done.1) | copy-start | bytes 4718596
where the time goes:
time: 106 us; the launch traced here: 105 us
  Pallas kernels  55.3 us (52%)
  starting transfers between devices  30.3 us (29%)
  local copies, waits for them, and re-layouts  11.5 us (11%)
  waiting for transfers between devices  7.26 us (7%)
    all_to_all x2, starting transfers between devices, exchanged(): return lax.all_to_all(value, AXES, split_axis=0, concat_axis=0, tiled=True)  24.7 us
    pallas_call x1, Pallas kernels, near(): pl.pallas_call(near_kernel, grid_spec=pltpu.PrefetchScalarGridSpec(num_sc...  16.5 us
    pallas_call x1, Pallas kernels, operators(): pl.pallas_call(operators_kernel, grid=(blocks,), in_specs=[pl.BlockSpec((...  16 us
    pallas_call x1, Pallas kernels, downward(): pl.pallas_call(downward_kernel, grid=(boxes // 8,), in_specs=[pl.BlockSpe...  8.83 us
    pallas_call x1, Pallas kernels, upward(): pl.pallas_call(upward_kernel, grid=(parents,), in_specs=[pl.BlockSpec((2,...  8.38 us
    all_to_all x2, waiting for transfers between devices, exchanged(): return lax.all_to_all(value, AXES, split_axis=0, concat_axis=0, tiled=True)  7.25 us
    ppermute x2, starting transfers between devices, passed_along(): return lax.ppermute(value, axis, pairs)  5.55 us
    pallas_call x1, Pallas kernels, translate(): pl.pallas_call(translate_kernel, in_specs=[pl.BlockSpec(memory_space=pltp...  5.52 us
  transfers between devices with their start and end apart: 4, of which 1 were waited for; matrix products, arithmetic and copies ran while one was open for 9% of the time, Pallas kernels for 36%

commit v1 on v0

v1 whole, which is shorter than its diff:
```python
import jax
import jax.numpy as jnp
from jax import lax
from jax.experimental import pallas as pl
from jax.experimental.pallas import tpu as pltpu
from jax.sharding import PartitionSpec as P

BF16 = jnp.bfloat16
F32 = jnp.float32
AXES = ("box", "dir")
MIB = 1 << 20
OWNED = 3
CODE = 512
DEAD = 1023


def passed_along(value, axis, by):
    peers = lax.axis_size(axis)
    pairs = [(i, i + by) for i in range(peers) if 0 <= i + by < peers]
    return lax.ppermute(value, axis, pairs)


def dot(left, right):
    return jnp.dot(left, right, preferred_element_type=F32)


def embedded(real, imag):
    return jnp.concatenate(
        [jnp.concatenate([real, -imag], axis=1), jnp.concatenate([imag, real], axis=1)], axis=0
    )


def interleave(upper, lower):
    rows, columns = upper.shape
    a = upper.reshape(rows // 8, 8, columns)
    b = lower.reshape(rows // 8, 8, columns)
    first = lax.broadcasted_iota(jnp.int32, a.shape, 1) < 4
    t = jnp.where(first, a, pltpu.roll(b, 4, 1))
    u = jnp.where(first, pltpu.roll(a, 4, 1), b)
    return jnp.stack([t, u], axis=1).reshape(2 * rows, columns)


def separate(mixed):
    rows, columns = mixed.shape
    parts = mixed.reshape(rows // 16, 2, 8, columns)
    t, u = parts[:, 0], parts[:, 1]
    first = lax.broadcasted_iota(jnp.int32, t.shape, 1) < 4
    a = jnp.where(first, t, pltpu.roll(u, 4, 1))
    b = jnp.where(first, pltpu.roll(t, 4, 1), u)
    return jnp.concatenate([a, b], axis=0).reshape(rows, columns)


def upward_kernel(
    cur_hbm, rad_hbm, interp_ref, angle_ref, out_hbm, first_hbm, last_hbm,
    cur_ref, rad_ref, w_ref, leaf_ref, out_ref, in_sems, halo_sems, out_sems
):
    half = interp_ref.shape[0]
    boxes = cur_ref.shape[1]
    parents = boxes // 8
    reach = first_hbm.shape[1]
    pieces = out_sems.shape[1]
    piece = half // pieces

    def arrivals(p):
        of = pl.ds(p * 8, 8)
        return (
            pltpu.make_async_copy(cur_hbm.at[:, of], cur_ref.at[:, of], in_sems.at[p, 0]),
            pltpu.make_async_copy(rad_hbm.at[of], rad_ref.at[of], in_sems.at[p, 1]),
        )

    for copy in arrivals(0):
        copy.start()

    angle = angle_ref[...]
    cosine = jnp.cos(angle).T
    sine = jnp.sin(angle).T
    interp = interp_ref[...].astype(F32)
    for c in range(8):
        ci = (cosine[:, c : c + 1] * interp).astype(BF16)
        si = (sine[:, c : c + 1] * interp).astype(BF16)
        left = slice(c * 256, c * 256 + 128)
        right = slice(c * 256 + 128, c * 256 + 256)
        for n in range(pieces):
            rows = slice(n * piece, (n + 1) * piece)
            real = slice(2 * n * piece, (2 * n + 1) * piece)
            imag = slice((2 * n + 1) * piece, (2 * n + 2) * piece)
            w_ref[real, left] = ci[rows]
            w_ref[real, right] = -si[rows]
            w_ref[imag, left] = si[rows]
            w_ref[imag, right] = ci[rows]

    def departures(p):
        lanes = pl.ds(pl.multiple_of(p * 256, 256), 256)
        copies = []
        for n in range(pieces):
            rows = pl.ds(2 * n * piece, 2 * piece)
            copies.append(
                pltpu.make_async_copy(
                    out_ref.at[p, rows], out_hbm.at[rows, lanes], out_sems.at[p, n]
                )
            )
        return copies

    halos = []
    for n, (start, target) in enumerate(((0, first_hbm), (boxes - reach, last_hbm))):
        source = cur_ref.at[:, pl.ds(start, reach)]
        halos.append(pltpu.make_async_copy(source, target, halo_sems.at[n]))

    def body(p, carry):
        for copy in arrivals(p):
            copy.wait()

        @pl.when(p + 1 < parents)
        def _():
            for copy in arrivals(p + 1):
                copy.start()

        @pl.when(p + 1 == parents)
        def _():
            for copy in halos:
                copy.start()

        for c in range(8):
            box = p * 8 + c
            x = cur_ref[:, box].reshape(256, 256)
            leaf = dot(embedded(rad_ref[box, 0], rad_ref[box, 1]), x)
            leaf_ref[c * 256 : (c + 1) * 256, :] = leaf.astype(BF16)
        for n, copy in enumerate(departures(p)):
            rows = slice(2 * n * piece, (2 * n + 2) * piece)
            y = dot(w_ref[rows], leaf_ref[...])
            out_ref[p, rows, :] = interleave(y[:piece], y[piece:]).astype(BF16)
            copy.start()
        return carry

    lax.fori_loop(0, parents, body, 0)
    for p in range(parents):
        for copy in departures(p):
            copy.wait()
    for copy in halos:
        copy.wait()


def upward(currents, radiate, interp, angle):
    parts, boxes, unknowns, columns = currents.shape
    parents = boxes // 8
    directions = interp.shape[0]
    sent = (2 * directions, parents * columns)
    halo = jax.ShapeDtypeStruct((parts, boxes // 2, unknowns, columns), BF16)
    return pl.pallas_call(
        upward_kernel,
        in_specs=[
            pl.BlockSpec(memory_space=pltpu.HBM),
            pl.BlockSpec(memory_space=pltpu.HBM),
            pl.BlockSpec(memory_space=pltpu.VMEM),
            pl.BlockSpec(memory_space=pltpu.VMEM),
        ],
        out_specs=[pl.BlockSpec(memory_space=pl.ANY)] * 3,
        out_shape=[jax.ShapeDtypeStruct(sent, BF16), halo, halo],
        scratch_shapes=[
            pltpu.VMEM(currents.shape, BF16),
            pltpu.VMEM(radiate.shape, BF16),
            pltpu.VMEM((2 * directions, 2048), BF16),
            pltpu.VMEM((2048, 256), BF16),
            pltpu.VMEM((parents, 2 * directions, columns), BF16),
            pltpu.SemaphoreType.DMA((parents, 2)),
            pltpu.SemaphoreType.DMA((2,)),
            pltpu.SemaphoreType.DMA((parents, 2)),
        ],
        compiler_params=pltpu.CompilerParams(vmem_limit_bytes=60 * MIB),
        cost_estimate=pl.CostEstimate(flops=5_000_000_000, bytes_accessed=7_000_000, transcendentals=0),
        name="upward",
    )(currents, radiate, interp, angle)


def iota(shape, axis):
    return lax.broadcasted_iota(jnp.int32, shape, axis)


def operators_kernel(far_ref, trans_ref, count_ref, table_ref, out_ref, code_ref, wide_ref, mask_ref):
    slots, parents = far_ref.shape
    blocks, width = code_ref.shape
    owned = OWNED
    devices = parents // owned
    per = blocks // owned

    def device(p):
        return (p * (65536 // owned + 1)) >> 16

    far = far_ref[...]
    source = (far - device(far) * owned) * devices + device(far)
    live = iota(far.shape, 0) < count_ref[...]
    code = jnp.where(live, source, DEAD) * CODE + trans_ref[...]
    lane = iota((1, width), 1)
    owner = lane // slots
    spread = jnp.where(iota((slots, width), 0) == lane - owner * slots, 1.0, 0.0)
    exact = dict(precision=lax.Precision.HIGHEST, preferred_element_type=F32)
    flat = jnp.dot(code.astype(F32).T, spread, **exact)
    flat = jnp.where((device(iota((parents, 1), 0)) & 15) == owner, flat, 0.0)
    p = iota((1, parents), 1)
    block = (p - device(p) * owned) * per + (device(p) >> 4)
    member = jnp.where(iota((blocks, parents), 0) == block, 1.0, 0.0)
    code_ref[...] = jnp.dot(member, flat, **exact).astype(jnp.int32)
    table = table_ref[...]
    wide = jnp.broadcast_to(table[:, None, :], (8, 16, table.shape[1]))
    wide_ref[...] = wide.reshape(128, table.shape[1]).astype(BF16)
    mask_ref[...] = jnp.where((iota((128, 1), 0) & 15) == owner, 1.0, 0.0).astype(BF16)

    def picks(size, index):
        return jnp.where(iota((size, width), 0) == index, 1.0, 0.0).astype(BF16)

    def body(i, carry):
        code = code_ref[pl.ds(i, 1), :]
        factor = dot(wide_ref[...], picks(wide_ref.shape[1], code & (CODE - 1)))
        factor = factor.astype(BF16) * mask_ref[...]
        matrix = lax.dot_general(
            factor,
            picks(parents, code >> 9),
            (((1,), (1,)), ((), ())),
            preferred_element_type=F32,
        )
        rows = pl.ds(pl.multiple_of(i * 16, 16), 16)
        out_ref[:, rows, :] = matrix.reshape(8, 16, parents).astype(BF16)
        return carry

    lax.fori_loop(0, blocks, body, 0, unroll=2)


def operators(far, trans, count, table):
    slots, parents = far.shape
    blocks = parents // 16
    return pl.pallas_call(
        operators_kernel,
        in_specs=[pl.BlockSpec(memory_space=pltpu.VMEM)] * 4,
        out_specs=pl.BlockSpec(memory_space=pltpu.VMEM),
        out_shape=jax.ShapeDtypeStruct((8, parents, parents), BF16),
        scratch_shapes=[
            pltpu.VMEM((blocks, 16 * slots), jnp.int32),
            pltpu.VMEM((128, table.shape[1]), BF16),
            pltpu.VMEM((128, 16 * slots), BF16),
        ],
        compiler_params=pltpu.CompilerParams(vmem_limit_bytes=32 * MIB),
        cost_estimate=pl.CostEstimate(flops=12_000_000_000, bytes_accessed=3_000_000, transcendentals=0),
        name="operators",
    )(far, trans, count, table)


def translate_kernel(x_hbm, m_ref, out_ref, x_ref, xp_ref, yp_ref, sems):
    groups = 4
    rows = x_ref.shape[0] // groups
    share = rows // 8
    owned = x_ref.shape[1] // 256
    parents = m_ref.shape[1]
    copies = []
    for g in range(groups):
        of = pl.ds(g * rows, rows)
        copies.append(pltpu.make_async_copy(x_hbm.at[of], x_ref.at[of], sems.at[g]))
    copies[0].start()
    copies[1].start()
    row, column = iota((rows, rows), 0), iota((rows, rows), 1)
    gather = jnp.where(column == (row & (share - 1)) * 8 + (row // share), 1.0, 0.0).astype(BF16)
    scatter = jnp.where(column == (row & 7) * share + (row >> 3), 1.0, 0.0).astype(BF16)
    for g in range(groups):
        copies[g].wait()
        if g + 2 < groups:
            copies[g + 2].start()
        xp_ref[g] = dot(gather, x_ref[g * rows : (g + 1) * rows, :]).astype(BF16)
    for j in range(4):
        x = jnp.concatenate(
            [
                xp_ref[g, (c * 4 + j) * share : (c * 4 + j + 1) * share, p * 256 : (p + 1) * 256]
                for c in range(2)
                for p in range(owned)
                for g in range(groups)
            ],
            axis=0,
        )
        y = dot(embedded(m_ref[2 * j], m_ref[2 * j + 1]), x).astype(BF16)
        for c in range(2):
            for p in range(owned):
                for g in range(groups):
                    start = c * parents + (p * groups + g) * share
                    yp_ref[
                        g, (c * 4 + j) * share : (c * 4 + j + 1) * share, p * 256 : (p + 1) * 256
                    ] = y[start : start + share]
    for g in range(groups):
        out_ref[g * rows : (g + 1) * rows, :] = dot(scatter, yp_ref[g]).astype(BF16)


def translate(x, matrix):
    rows, width = x.shape
    return pl.pallas_call(
        translate_kernel,
        in_specs=[pl.BlockSpec(memory_space=pltpu.HBM), pl.BlockSpec(memory_space=pltpu.VMEM)],
        out_specs=pl.BlockSpec(memory_space=pltpu.VMEM),
        out_shape=jax.ShapeDtypeStruct(x.shape, BF16),
        scratch_shapes=[
            pltpu.VMEM(x.shape, BF16),
            pltpu.VMEM((4, rows // 4, width), BF16),
            pltpu.VMEM((4, rows // 4, width), BF16),
            pltpu.SemaphoreType.DMA((4,)),
        ],
        compiler_params=pltpu.CompilerParams(vmem_limit_bytes=32 * MIB),
        cost_estimate=pl.CostEstimate(flops=1_200_000_000, bytes_accessed=5_500_000, transcendentals=0),
        name="translate",
    )(pltpu.with_memory_space_constraint(x, pltpu.HBM), matrix)


def near_kernel(index_ref, count_ref, low_ref, cur_ref, up_ref, tile_ref, out_ref, win_ref, sems):
    step = pl.program_id(0)
    group, slots = tile_ref.shape[:2]
    reach = low_ref.shape[1]
    boxes = cur_ref.shape[1]

    @pl.when(step == 0)
    def _():
        copies = []
        for c in range(2):
            rows = pl.ds(c * 128, 128)
            starts = ((low_ref, 0, reach), (cur_ref, reach, boxes), (up_ref, reach + boxes, reach))
            for n, (source, start, size) in enumerate(starts):
                copies.append(
                    pltpu.make_async_copy(
                        source.at[c], win_ref.at[pl.ds(start, size), rows, :], sems.at[c * 3 + n]
                    )
                )
        for copy in copies:
            copy.start()
        for copy in copies:
            copy.wait()

    @pl.loop(0, group)
    def _(i):
        box = step * group + i
        for live in range(1, slots + 1):

            @pl.when(count_ref[box] == live)
            def _():
                tiles = [embedded(tile_ref[i, s, 0], tile_ref[i, s, 1]) for s in range(live)]
                picked = [win_ref[index_ref[box * slots + s]] for s in range(live)]
                out_ref[i] = dot(
                    jnp.concatenate(tiles, axis=1), jnp.concatenate(picked, axis=0)
                ).astype(out_ref.dtype)


def near(index, count, low, currents, up, tiles):
    boxes, slots = tiles.shape[:2]
    reach = low.shape[1]
    group = 4
    return pl.pallas_call(
        near_kernel,
        grid_spec=pltpu.PrefetchScalarGridSpec(
            num_scalar_prefetch=2,
            grid=(boxes // group,),
            in_specs=[
                pl.BlockSpec(memory_space=pl.ANY),
                pl.BlockSpec(memory_space=pl.ANY),
                pl.BlockSpec(memory_space=pl.ANY),
                pl.BlockSpec((group, slots, 2, 128, 128), lambda b, i, n: (b, 0, 0, 0, 0)),
            ],
            out_specs=pl.BlockSpec((group, 256, 256), lambda b, i, n: (b, 0, 0)),
            scratch_shapes=[
                pltpu.VMEM((boxes + 2 * reach, 256, 256), BF16),
                pltpu.SemaphoreType.DMA((6,)),
            ],
        ),
        out_shape=pltpu.HBM((boxes, 256, 256), BF16),
        compiler_params=pltpu.CompilerParams(vmem_limit_bytes=60 * MIB),
        cost_estimate=pl.CostEstimate(flops=7_200_000_000, bytes_accessed=27_000_000, transcendentals=0),
        name="near",
    )(index, count, low, currents, up, tiles)


def downward_kernel(
    z_ref, interp_ref, angle_ref, rec_hbm, near_hbm, out_hbm,
    rec_ref, near_ref, w_ref, arr_ref, out_ref, in_sems, out_sems
):
    half = angle_ref.shape[1]
    parents = z_ref.shape[1] // 256
    coming = []
    for p in range(parents):
        of = pl.ds(p * 8, 8)
        coming.append(
            (
                pltpu.make_async_copy(rec_hbm.at[of], rec_ref.at[of], in_sems.at[p, 0]),
                pltpu.make_async_copy(near_hbm.at[of], near_ref.at[of], in_sems.at[p, 1]),
            )
        )
    for copy in coming[0]:
        copy.start()
    angle = angle_ref[...]
    cosine = jnp.cos(angle)
    sine = jnp.sin(angle)
    interp = interp_ref[...].astype(F32).T

    def matrix(c):
        ci = (cosine[c : c + 1] * interp).astype(BF16)
        si = (sine[c : c + 1] * interp).astype(BF16)
        w_ref[c * 256 : c * 256 + 128, :half] = ci
        w_ref[c * 256 : c * 256 + 128, half:] = si
        w_ref[c * 256 + 128 : c * 256 + 256, :half] = -si
        w_ref[c * 256 + 128 : c * 256 + 256, half:] = ci

    going = []
    for p in range(parents):
        z = separate(z_ref[:, p * 256 : (p + 1) * 256].astype(F32)).astype(BF16)
        pieces = 4 if p == 0 else 1
        for n in range(pieces):
            if p == 0:
                for c in range(n * 8 // pieces, (n + 1) * 8 // pieces):
                    matrix(c)
            rows = slice(n * 2048 // pieces, (n + 1) * 2048 // pieces)
            arr_ref[p % 2, rows, :] = dot(w_ref[rows, :], z).astype(BF16)
        for copy in coming[p]:
            copy.wait()
        if p + 1 < parents:
            for copy in coming[p + 1]:
                copy.start()
        for c in range(8):
            box = p * 8 + c
            arriving = arr_ref[p % 2, c * 256 : (c + 1) * 256, :]
            far = dot(embedded(rec_ref[box, 0], rec_ref[box, 1]), arriving)
            out_ref[:, box] = (far + near_ref[box].astype(F32)).astype(BF16).reshape(2, 128, 256)
            if c % 4 == 3:
                of = pl.ds(box - 3, 4)
                going.append(
                    pltpu.make_async_copy(
                        out_ref.at[:, of], out_hbm.at[:, of], out_sems.at[box // 4]
                    )
                )
                going[-1].start()
    for copy in going:
        copy.wait()


def downward(z, interp, angle, receive, near_field):
    boxes = receive.shape[0]
    response = (2, boxes, 128, 256)
    return pl.pallas_call(
        downward_kernel,
        in_specs=[pl.BlockSpec(memory_space=pltpu.VMEM)] * 3
        + [pl.BlockSpec(memory_space=pltpu.HBM)] * 2,
        out_specs=pl.BlockSpec(memory_space=pltpu.HBM),
        out_shape=jax.ShapeDtypeStruct(response, BF16),
        scratch_shapes=[
            pltpu.VMEM(receive.shape, BF16),
            pltpu.VMEM(near_field.shape, BF16),
            pltpu.VMEM((2048, 2 * interp.shape[0]), BF16),
            pltpu.VMEM((2, 2048, 256), BF16),
            pltpu.VMEM(response, BF16),
            pltpu.SemaphoreType.DMA((boxes // 8, 2)),
            pltpu.SemaphoreType.DMA((boxes // 4,)),
        ],
        compiler_params=pltpu.CompilerParams(vmem_limit_bytes=32 * MIB),
        cost_estimate=pl.CostEstimate(flops=5_000_000_000, bytes_accessed=13_000_000, transcendentals=0),
        name="downward",
    )(
        z,
        interp,
        angle,
        pltpu.with_memory_space_constraint(receive, pltpu.HBM),
        pltpu.with_memory_space_constraint(near_field, pltpu.HBM),
    )


def exchanged(value):
    return lax.all_to_all(value, AXES, split_axis=0, concat_axis=0, tiled=True)


def local(
    currents,
    near_tiles,
    near_index,
    near_count,
    radiate,
    receive,
    interp,
    shift_angle,
    far_index,
    far_count,
    trans_index,
    translators,
):
    boxes = currents.shape[1]
    reach = boxes // 2
    sent, leading, trailing = upward(currents, radiate, interp, shift_angle)
    by_direction = exchanged(sent)
    lower = passed_along(trailing, AXES, 1)
    upper = passed_along(leading, AXES, -1)

    table = translators.transpose(2, 1, 0).reshape(8, -1)
    table = jnp.pad(table, ((0, 0), (0, -table.shape[1] % 128)))
    matrix = operators(far_index.T, trans_index.T, far_count[None, :], table)

    back = translate(by_direction, matrix)
    incoming = exchanged(back)

    first = lax.axis_index(AXES) * boxes - reach
    near_field = near(
        (near_index - first).reshape(-1), near_count, lower, currents, upper, near_tiles
    )
    return downward(incoming, interp, shift_angle, receive, near_field)


def solution(mesh):
    placed = (
        P(None, AXES, None, None),
        P(AXES, None, None, None, None),
        P(AXES, None),
        P(AXES),
        P(AXES, None, None, None),
        P(AXES, None, None, None),
        P(),
        P(),
        P(),
        P(),
        P(),
        P(None, None, AXES),
    )
    return jax.shard_map(
        local,
        mesh=mesh,
        in_specs=placed,
        out_specs=P(None, AXES, None, None),
        check_vma=False,
    )
```

time: 106 us -> 88.9 us (0.84)
  local copies, waits for them, and re-layouts: 11.5 us -> 0.84 us
  starting transfers between devices: 30.3 us -> 22.4 us
  waiting for transfers between devices: 7.26 us -> 13.7 us
  Pallas kernels: 55.3 us -> 51 us
    all_to_all x2, starting transfers between devices: 24.7 us -> 16.9 us  [exchanged(): return lax.all_to_all(value, AXES, split_axis=0, concat_axis=0, tiled=True)]
    all_to_all x2, waiting for transfers between devices: 7.25 us -> 13.7 us  [exchanged(): return lax.all_to_all(value, AXES, split_axis=0, concat_axis=0, tiled=True)]
    pallas_call x3, Pallas kernels: 33.3 us -> 28.1 us  [the longest x1 11.4 us: operators(): pl.pallas_call(operators_kernel, in_specs=[pl.BlockSpec(memory_space=pltp...]
    slice x1 -> x0, local copies, waits for them, and re-layouts: 3.45 us -> none  [local(): upper = passed_along(currents[:, :reach], AXES, -1)]
    reshape x2 -> x1, local copies, waits for them, and re-layouts: 2.75 us -> 0.01 us  [local(): table = translators.transpose(2, 1, 0).reshape(8, -1)]
    unnamed x14, local copies, waits for them, and re-layouts: 2.33 us -> 0.04 us
  transfers between devices with their start and end apart: 4 -> 4, of which waited for: 1 -> 2; matrix products, arithmetic and copies ran while one was open for 9% -> 1% of each run, Pallas kernels for 36% -> 39%
where the time goes in v1:
time: 88.9 us; the launch traced here: 88.2 us
  Pallas kernels  51 us (57%)
  starting transfers between devices  22.4 us (25%)
  waiting for transfers between devices  13.7 us (15%)
    pallas_call x1, Pallas kernels, near(): pl.pallas_call(near_kernel, grid_spec=pltpu.PrefetchScalarGridSpec(num_sc...  17.4 us
    all_to_all x2, starting transfers between devices, exchanged(): return lax.all_to_all(value, AXES, split_axis=0, concat_axis=0, tiled=True)  16.9 us
    all_to_all x2, waiting for transfers between devices, exchanged(): return lax.all_to_all(value, AXES, split_axis=0, concat_axis=0, tiled=True)  13.7 us
    pallas_call x1, Pallas kernels, operators(): pl.pallas_call(operators_kernel, in_specs=[pl.BlockSpec(memory_space=pltp...  11.4 us
    pallas_call x1, Pallas kernels, downward(): pl.pallas_call(downward_kernel, in_specs=[pl.BlockSpec(memory_space=pltpu...  8.76 us
    pallas_call x1, Pallas kernels, upward(): pl.pallas_call(upward_kernel, in_specs=[pl.BlockSpec(memory_space=pltpu.H...  7.88 us
    pallas_call x1, Pallas kernels, translate(): pl.pallas_call(translate_kernel, in_specs=[pl.BlockSpec(memory_space=pltp...  5.51 us
    ppermute x2, starting transfers between devices, passed_along(): return lax.ppermute(value, axis, pairs)  5.48 us
  transfers between devices with their start and end apart: 4, of which 2 were waited for; matrix products, arithmetic and copies ran while one was open for 1% of the time, Pallas kernels for 39%

profile of v1, /device:TPU:1, one launch (start us, length us, event | category | flops | bytes accessed | tf_op | source)
XLA Modules:
  0.0 88.2 jit_solution(10704012052113175598)
XLA Ops:
  0.0 7.9 %upward.1 = (bf16[1024,768]{1,0:T(8,128)(2,1)}, bf16[2,12,128,256]{3,2,1,0:T(8,128)(2,1)}, bf16[2,12,128,256]{3,2,1,0:T(8,128)(2,1)}) custom-call(bf16[2,24,128,256]{3,2,1,0:T(8,128)(2,1)} %cur_ref.1, bf16[24,2,128,128]{3,2,1,0:T(8,128)(2,1)} %rad_hbm.1, bf16[512,128]{1,0:T(8,128)(2,1)} %interp_ref.3, f32[8,512]{1,0:T(8,128)} %angle_ref.3), custom_call_target="tpu_custom_call" | custom-call | flops 5000000000 | bytes 7000000 | tf_op jit(solution)/shard_map/upward/pallas_call | solution.py:149
  7.9 0.0 copy-start.4
  7.9 0.0 copy-start.6
  7.9 0.0 copy-start.1
  7.9 0.0 copy-start.2
  7.9 11.9 %all-to-all-start = ((bf16[128,8,768]{2,1,0:T(8,128)(2,1)}), bf16[128,8,768]{2,1,0:T(8,128)(2,1)}, u32[]{:S(2)}, u32[]{:S(2)}) async-start(bf16[128,8,768]{2,1,0:T(8,128)(2,1)} %bitcast.10), calls=%async_computation | async-start | bytes 3145728 | tf_op jit(solution)/shard_map/all_to_all | solution.py:466
  19.9 3.5 %collective-permute-start = (bf16[2,12,128,256]{3,2,1,0:T(8,128)(2,1)}, bf16[2,12,128,256]{3,2,1,0:T(8,128)(2,1)}, u32[]{:S(2)}, u32[]{:S(2)}) collective-permute-start(bf16[2,12,128,256]{3,2,1,0:T(8,128)(2,1)} %get-tuple-element.9), channel_id=1, source_target_pairs={{0,1},{1,2},{2,3},{3,4},{4,5},{5,6},{6,7},{7,8},{8,9},{9,10},{10,1... | collective-permute-start | bytes 4718600 | tf_op jit(solution)/shard_map/ppermute | solution.py:20
  23.4 1.9 %collective-permute-start.1 = (bf16[2,12,128,256]{3,2,1,0:T(8,128)(2,1)}, bf16[2,12,128,256]{3,2,1,0:T(8,128)(2,1)}, u32[]{:S(2)}, u32[]{:S(2)}) collective-permute-start(bf16[2,12,128,256]{3,2,1,0:T(8,128)(2,1)} %get-tuple-element.10), channel_id=1, source_target_pairs={{1,0},{2,1},{3,2},{4,3},{5,4},{6,5},{7,6},{8,7},{9,8},{10,9},{11,1... | collective-permute-start | bytes 4718600 | tf_op jit(solution)/shard_map/ppermute | solution.py:20
  25.3 0.0 copy-done.4
  25.4 0.0 copy-done.6
  25.4 0.0 copy-done.1
  25.4 0.0 copy-done.2
  25.4 11.4 %operators.1.m_ref = bf16[8,384,384]{2,1,0:T(8,128)(2,1)S(1)} custom-call(s32[48,384]{1,0:T(8,128)S(1)} %bitcast.8, s32[48,384]{1,0:T(8,128)S(1)} %bitcast.9, s32[1,384]{1,0:T(1,128)S(1)} %broadcast_in_dim.3.count_ref, f32[8,384]{1,0:T(8,128)S(1)} %pad.4.table_ref), custom_call_target="tpu_custom_call" | custom-call | flops 12000000000 | bytes 3000000 | tf_op jit(solution)/shard_map/operators/pallas_call | solution.py:231
  36.9 7.2 %all-to-all-done = bf16[128,8,768]{2,1,0:T(8,128)(2,1)} async-done(((bf16[128,8,768]{2,1,0:T(8,128)(2,1)}), bf16[128,8,768]{2,1,0:T(8,128)(2,1)}, u32[]{:S(2)}, u32[]{:S(2)}) %all-to-all-start) | async-done | bytes 1572896 | tf_op jit(solution)/shard_map/all_to_all | solution.py:466
  44.1 5.5 %translate.1 = bf16[1024,768]{1,0:T(8,128)(2,1)} custom-call(bf16[1024,768]{1,0:T(8,128)(2,1)} %bitcast.1.x_hbm, bf16[8,384,384]{2,1,0:T(8,128)(2,1)S(1)} %operators.1.m_ref), custom_call_target="tpu_custom_call" | custom-call | flops 1200000000 | bytes 5500000 | tf_op jit(solution)/shard_map/translate/pallas_call | solution.py:291
  49.6 0.0 copy-start.5
  49.6 5.0 %all-to-all-start.1 = ((bf16[128,8,768]{2,1,0:T(8,128)(2,1)}), bf16[128,8,768]{2,1,0:T(8,128)(2,1)S(1)}, u32[]{:S(2)}, u32[]{:S(2)}) async-start(bf16[128,8,768]{2,1,0:T(8,128)(2,1)} %bitcast.5), calls=%async_computation.1 | async-start | bytes 3145728 | tf_op jit(solution)/shard_map/all_to_all | solution.py:466
  54.6 0.0 copy-done.5
  54.7 0.1 copy.15
  54.7 0.7 reshape.11.index_ref
  55.4 0.0 copy-start
  55.4 0.0 copy-start.3
  55.4 0.0 collective-permute-done.low_ref
  55.4 0.0 collective-permute-done.1.up_ref
  55.4 17.4 %near.1.near_hbm = bf16[24,256,256]{2,1,0:T(8,128)(2,1)} custom-call(s32[216]{0:T(256)} %reshape.11.index_ref, s32[24]{0:T(128)} %count_ref.1, bf16[2,12,128,256]{3,2,1,0:T(8,128)(2,1)} %collective-permute-done.low_ref, bf16[2,24,128,256]{3,2,1,0:T(8,128)(2,1)} %cur_ref.1, bf16[2,12,128,256]{3,2,1,0:T(8,128)(2,1)} %collective-permute-done.1.up_ref, ...), custom_call_target="tpu_custom_call" | custom-call | flops 7200000000 | bytes 27000000 | tf_op jit(solution)/shard_map/near/pallas_call | solution.py:349
  72.8 6.5 %all-to-all-done.1 = bf16[128,8,768]{2,1,0:T(8,128)(2,1)S(1)} async-done(((bf16[128,8,768]{2,1,0:T(8,128)(2,1)}), bf16[128,8,768]{2,1,0:T(8,128)(2,1)S(1)}, u32[]{:S(2)}, u32[]{:S(2)}) %all-to-all-start.1) | async-done | bytes 1572896 | tf_op jit(solution)/shard_map/all_to_all | solution.py:466
  79.3 0.0 copy-done
  79.3 0.0 copy-done.3
  79.3 8.8 %downward.1 = bf16[2,24,128,256]{3,2,1,0:T(8,128)(2,1)} custom-call(bf16[1024,768]{1,0:T(8,128)(2,1)S(1)} %bitcast.7, bf16[512,128]{1,0:T(8,128)(2,1)S(1)} %copy-done, f32[8,512]{1,0:T(8,128)S(1)} %copy-done.3, bf16[24,2,128,128]{3,2,1,0:T(8,128)(2,1)} %rec_hbm.1, bf16[24,256,256]{2,1,0:T(8,128)(2,1)} %near.1.near_hbm), custom_call_target="tpu_custom_call" | custom-call | flops 5000000000 | bytes 13000000 | tf_op jit(solution)/shard_map/downward/pallas_call | solution.py:438
  (5 shorter events, 0.0 us)
Async XLA Ops:
  7.9 17.5 %copy-start.4 = (f32[316,2,4]{0,2,1:T(4,128)S(1)}, f32[316,2,4]{0,2,1:T(4,128)}, u32[]{:S(2)}) copy-start(f32[316,2,4]{0,2,1:T(4,128)} %param.23) | copy-start | bytes 30340
  7.9 17.5 %copy-start.6 = (s32[384]{0:T(512)S(1)}, s32[384]{0:T(512)}, u32[]{:S(2)}) copy-start(s32[384]{0:T(512)} %param.21) | copy-start | bytes 4612
  7.9 17.5 %copy-start.1 = (s32[384,48]{0,1:T(8,128)S(1)}, s32[384,48]{0,1:T(8,128)}, u32[]{:S(2)}) copy-start(s32[384,48]{0,1:T(8,128)} %param.20) | copy-start | bytes 221188
  7.9 17.5 %copy-start.2 = (s32[384,48]{0,1:T(8,128)S(1)}, s32[384,48]{0,1:T(8,128)}, u32[]{:S(2)}) copy-start(s32[384,48]{0,1:T(8,128)} %param.22) | copy-start | bytes 221188
  7.9 36.2 %all-to-all-start = ((bf16[128,8,768]{2,1,0:T(8,128)(2,1)}), bf16[128,8,768]{2,1,0:T(8,128)(2,1)}, u32[]{:S(2)}, u32[]{:S(2)}) async-start(bf16[128,8,768]{2,1,0:T(8,128)(2,1)} %bitcast.10), calls=%async_computation | async-start | bytes 3145728 | tf_op jit(solution)/shard_map/all_to_all | solution.py:466
  19.9 35.6 %collective-permute-start = (bf16[2,12,128,256]{3,2,1,0:T(8,128)(2,1)}, bf16[2,12,128,256]{3,2,1,0:T(8,128)(2,1)}, u32[]{:S(2)}, u32[]{:S(2)}) collective-permute-start(bf16[2,12,128,256]{3,2,1,0:T(8,128)(2,1)} %get-tuple-element.9), channel_id=1, source_target_pairs={{0,1},{1,2},{2,3},{3,4},{4,5},{5,6},{6,7},{7,8},{8,9},{9,10},{10,1... | collective-permute-start | bytes 4718600 | tf_op jit(solution)/shard_map/ppermute | solution.py:20
  23.4 32.0 %collective-permute-start.1 = (bf16[2,12,128,256]{3,2,1,0:T(8,128)(2,1)}, bf16[2,12,128,256]{3,2,1,0:T(8,128)(2,1)}, u32[]{:S(2)}, u32[]{:S(2)}) collective-permute-start(bf16[2,12,128,256]{3,2,1,0:T(8,128)(2,1)} %get-tuple-element.10), channel_id=1, source_target_pairs={{1,0},{2,1},{3,2},{4,3},{5,4},{6,5},{7,6},{8,7},{9,8},{10,9},{11,1... | collective-permute-start | bytes 4718600 | tf_op jit(solution)/shard_map/ppermute | solution.py:20
  49.6 5.0 %copy-start.5 = (s32[24,9]{0,1:T(8,128)S(1)}, s32[24,9]{0,1:T(8,128)}, u32[]{:S(2)}) copy-start(s32[24,9]{0,1:T(8,128)} %param.14) | copy-start | bytes 2596
  49.6 29.7 %all-to-all-start.1 = ((bf16[128,8,768]{2,1,0:T(8,128)(2,1)}), bf16[128,8,768]{2,1,0:T(8,128)(2,1)S(1)}, u32[]{:S(2)}, u32[]{:S(2)}) async-start(bf16[128,8,768]{2,1,0:T(8,128)(2,1)} %bitcast.5), calls=%async_computation.1 | async-start | bytes 3145728 | tf_op jit(solution)/shard_map/all_to_all | solution.py:466
  55.4 23.9 %copy-start = (bf16[512,128]{1,0:T(8,128)(2,1)S(1)}, bf16[512,128]{1,0:T(8,128)(2,1)}, u32[]{:S(2)}) copy-start(bf16[512,128]{1,0:T(8,128)(2,1)} %interp_ref.3) | copy-start | bytes 393220
  55.4 23.9 %copy-start.3 = (f32[8,512]{1,0:T(8,128)S(1)}, f32[8,512]{1,0:T(8,128)}, u32[]{:S(2)}) copy-start(f32[8,512]{1,0:T(8,128)} %angle_ref.3) | copy-start | bytes 49156

commit v2 on v1

--- a/solution.py
+++ b/solution.py
@@ -176,7 +176,9 @@
     return lax.broadcasted_iota(jnp.int32, shape, axis)
 
 
-def operators_kernel(far_ref, trans_ref, count_ref, table_ref, out_ref, code_ref, wide_ref, mask_ref):
+def operators_kernel(
+    far_ref, trans_ref, count_ref, table_ref, out_ref, rest_hbm, code_ref, wide_ref, mask_ref, rest_ref, sem
+):
     slots, parents = far_ref.shape
     blocks, width = code_ref.shape
     owned = OWNED
@@ -219,10 +221,15 @@
             preferred_element_type=F32,
         )
         rows = pl.ds(pl.multiple_of(i * 16, 16), 16)
-        out_ref[:, rows, :] = matrix.reshape(8, 16, parents).astype(BF16)
+        matrix = matrix.reshape(8, 16, parents).astype(BF16)
+        out_ref[:, rows, :] = matrix[:4]
+        rest_ref[:, rows, :] = matrix[4:]
         return carry
 
     lax.fori_loop(0, blocks, body, 0, unroll=2)
+    copy = pltpu.make_async_copy(rest_ref, rest_hbm, sem.at[0])
+    copy.start()
+    copy.wait()
 
 
 def operators(far, trans, count, table):
@@ -231,12 +238,17 @@
     return pl.pallas_call(
         operators_kernel,
         in_specs=[pl.BlockSpec(memory_space=pltpu.VMEM)] * 4,
-        out_specs=pl.BlockSpec(memory_space=pltpu.VMEM),
-        out_shape=jax.ShapeDtypeStruct((8, parents, parents), BF16),
+        out_specs=[pl.BlockSpec(memory_space=pltpu.VMEM), pl.BlockSpec(memory_space=pltpu.HBM)],
+        out_shape=[
+            jax.ShapeDtypeStruct((4, parents, parents), BF16),
+            pltpu.HBM((4, parents, parents), BF16),
+        ],
         scratch_shapes=[
             pltpu.VMEM((blocks, 16 * slots), jnp.int32),
             pltpu.VMEM((128, table.shape[1]), BF16),
             pltpu.VMEM((128, 16 * slots), BF16),
+            pltpu.VMEM((4, parents, parents), BF16),
+            pltpu.SemaphoreType.DMA((1,)),
         ],
         compiler_params=pltpu.CompilerParams(vmem_limit_bytes=32 * MIB),
         cost_estimate=pl.CostEstimate(flops=12_000_000_000, bytes_accessed=3_000_000, transcendentals=0),
@@ -244,27 +256,23 @@
     )(far, trans, count, table)
 
 
-def translate_kernel(x_hbm, m_ref, out_ref, x_ref, xp_ref, yp_ref, sems):
+def translate_kernel(x_ref, m_ref, rest_hbm, out_ref, rest_ref, xp_ref, yp_ref, sem):
     groups = 4
     rows = x_ref.shape[0] // groups
     share = rows // 8
     owned = x_ref.shape[1] // 256
     parents = m_ref.shape[1]
-    copies = []
-    for g in range(groups):
-        of = pl.ds(g * rows, rows)
-        copies.append(pltpu.make_async_copy(x_hbm.at[of], x_ref.at[of], sems.at[g]))
-    copies[0].start()
-    copies[1].start()
+    copy = pltpu.make_async_copy(rest_hbm, rest_ref, sem.at[0])
+    copy.start()
     row, column = iota((rows, rows), 0), iota((rows, rows), 1)
     gather = jnp.where(column == (row & (share - 1)) * 8 + (row // share), 1.0, 0.0).astype(BF16)
     scatter = jnp.where(column == (row & 7) * share + (row >> 3), 1.0, 0.0).astype(BF16)
     for g in range(groups):
-        copies[g].wait()
-        if g + 2 < groups:
-            copies[g + 2].start()
         xp_ref[g] = dot(gather, x_ref[g * rows : (g + 1) * rows, :]).astype(BF16)
     for j in range(4):
+        if j == 2:
+            copy.wait()
+        from_ref = m_ref if j < 2 else rest_ref
         x = jnp.concatenate(
             [
                 xp_ref[g, (c * 4 + j) * share : (c * 4 + j + 1) * share, p * 256 : (p + 1) * 256]
@@ -274,7 +282,8 @@
             ],
             axis=0,
         )
-        y = dot(embedded(m_ref[2 * j], m_ref[2 * j + 1]), x).astype(BF16)
+        real, imag = from_ref[j % 2 * 2], from_ref[j % 2 * 2 + 1]
+        y = dot(embedded(real, imag), x).astype(BF16)
         for c in range(2):
             for p in range(owned):
                 for g in range(groups):
@@ -286,23 +295,24 @@
         out_ref[g * rows : (g + 1) * rows, :] = dot(scatter, yp_ref[g]).astype(BF16)
 
 
-def translate(x, matrix):
+def translate(x, matrix, rest):
     rows, width = x.shape
     return pl.pallas_call(
         translate_kernel,
-        in_specs=[pl.BlockSpec(memory_space=pltpu.HBM), pl.BlockSpec(memory_space=pltpu.VMEM)],
+        in_specs=[pl.BlockSpec(memory_space=pltpu.VMEM)] * 2
+        + [pl.BlockSpec(memory_space=pltpu.HBM)],
         out_specs=pl.BlockSpec(memory_space=pltpu.VMEM),
         out_shape=jax.ShapeDtypeStruct(x.shape, BF16),
         scratch_shapes=[
-            pltpu.VMEM(x.shape, BF16),
+            pltpu.VMEM(rest.shape, BF16),
             pltpu.VMEM((4, rows // 4, width), BF16),
             pltpu.VMEM((4, rows // 4, width), BF16),
-            pltpu.SemaphoreType.DMA((4,)),
+            pltpu.SemaphoreType.DMA((1,)),
         ],
         compiler_params=pltpu.CompilerParams(vmem_limit_bytes=32 * MIB),
         cost_estimate=pl.CostEstimate(flops=1_200_000_000, bytes_accessed=5_500_000, transcendentals=0),
         name="translate",
-    )(pltpu.with_memory_space_constraint(x, pltpu.HBM), matrix)
+    )(x, matrix, pltpu.with_memory_space_constraint(rest, pltpu.HBM))
 
 
 def near_kernel(index_ref, count_ref, low_ref, cur_ref, up_ref, tile_ref, out_ref, win_ref, sems):
@@ -403,7 +413,7 @@
     going = []
     for p in range(parents):
         z = separate(z_ref[:, p * 256 : (p + 1) * 256].astype(F32)).astype(BF16)
-        pieces = 4 if p == 0 else 1
+        pieces = 8
         for n in range(pieces):
             if p == 0:
                 for c in range(n * 8 // pieces, (n + 1) * 8 // pieces):
@@ -489,9 +499,9 @@
 
     table = translators.transpose(2, 1, 0).reshape(8, -1)
     table = jnp.pad(table, ((0, 0), (0, -table.shape[1] % 128)))
-    matrix = operators(far_index.T, trans_index.T, far_count[None, :], table)
-
-    back = translate(by_direction, matrix)
+    matrix, rest = operators(far_index.T, trans_index.T, far_count[None, :], table)
+
+    back = translate(by_direction, matrix, rest)
     incoming = exchanged(back)
 
     first = lax.axis_index(AXES) * boxes - reach

time: 88.9 us -> 85.6 us (0.963)
  Pallas kernels: 51 us -> 48.5 us
    pallas_call x1, Pallas kernels: 8.76 us -> 6.22 us  [downward(): pl.pallas_call(downward_kernel, in_specs=[pl.BlockSpec(memory_space=pltpu...]
    pallas_call x1, Pallas kernels: 11.4 us -> 12.5 us  [operators(): pl.pallas_call(operators_kernel, in_specs=[pl.BlockSpec(memory_space=pltp...]
  transfers between devices with their start and end apart: 4 -> 4, of which waited for: 2 -> 3; matrix products, arithmetic and copies ran while one was open for 1% -> 1% of each run, Pallas kernels for 39% -> 41%
where the time goes in v2:
time: 85.6 us; the launch traced here: 84.9 us
  Pallas kernels  48.5 us (57%)
  starting transfers between devices  21.9 us (26%)
  waiting for transfers between devices  13.3 us (16%)
    pallas_call x1, Pallas kernels, near(): pl.pallas_call(near_kernel, grid_spec=pltpu.PrefetchScalarGridSpec(num_sc...  17.1 us
    all_to_all x2, starting transfers between devices, exchanged(): return lax.all_to_all(value, AXES, split_axis=0, concat_axis=0, tiled=True)  16.5 us
    all_to_all x2, waiting for transfers between devices, exchanged(): return lax.all_to_all(value, AXES, split_axis=0, concat_axis=0, tiled=True)  13 us
    pallas_call x1, Pallas kernels, operators(): pl.pallas_call(operators_kernel, in_specs=[pl.BlockSpec(memory_space=pltp...  12.5 us
    pallas_call x1, Pallas kernels, upward(): pl.pallas_call(upward_kernel, in_specs=[pl.BlockSpec(memory_space=pltpu.H...  7.88 us
    pallas_call x1, Pallas kernels, downward(): pl.pallas_call(downward_kernel, in_specs=[pl.BlockSpec(memory_space=pltpu...  6.22 us
    ppermute x2, starting transfers between devices, passed_along(): return lax.ppermute(value, axis, pairs)  5.47 us
    pallas_call x1, Pallas kernels, translate(): pl.pallas_call(translate_kernel, in_specs=[pl.BlockSpec(memory_space=pltp...  4.85 us
  transfers between devices with their start and end apart: 4, of which 3 were waited for; matrix products, arithmetic and copies ran while one was open for 1% of the time, Pallas kernels for 41%

profile of v2, /device:TPU:1, one launch (start us, length us, event | category | flops | bytes accessed | tf_op | source)
XLA Modules:
  0.0 84.9 jit_solution(147333283939426491)
XLA Ops:
  0.0 7.9 %upward.1 = (bf16[1024,768]{1,0:T(8,128)(2,1)}, bf16[2,12,128,256]{3,2,1,0:T(8,128)(2,1)}, bf16[2,12,128,256]{3,2,1,0:T(8,128)(2,1)}) custom-call(bf16[2,24,128,256]{3,2,1,0:T(8,128)(2,1)} %cur_ref.1, bf16[24,2,128,128]{3,2,1,0:T(8,128)(2,1)} %rad_hbm.1, bf16[512,128]{1,0:T(8,128)(2,1)} %interp_ref.3, f32[8,512]{1,0:T(8,128)} %angle_ref.3), custom_call_target="tpu_custom_call" | custom-call | flops 5000000000 | bytes 7000000 | tf_op jit(solution)/shard_map/upward/pallas_call | solution.py:149
  7.9 0.0 copy-start.4
  7.9 0.0 copy-start.6
  7.9 0.0 copy-start.1
  7.9 0.0 copy-start.2
  7.9 11.5 %all-to-all-start = ((bf16[128,8,768]{2,1,0:T(8,128)(2,1)}), bf16[128,8,768]{2,1,0:T(8,128)(2,1)S(1)}, u32[]{:S(2)}, u32[]{:S(2)}) async-start(bf16[128,8,768]{2,1,0:T(8,128)(2,1)} %bitcast.11), calls=%async_computation | async-start | bytes 3145728 | tf_op jit(solution)/shard_map/all_to_all | solution.py:476
  19.4 3.5 %collective-permute-start = (bf16[2,12,128,256]{3,2,1,0:T(8,128)(2,1)}, bf16[2,12,128,256]{3,2,1,0:T(8,128)(2,1)}, u32[]{:S(2)}, u32[]{:S(2)}) collective-permute-start(bf16[2,12,128,256]{3,2,1,0:T(8,128)(2,1)} %get-tuple-element.13), channel_id=1, source_target_pairs={{0,1},{1,2},{2,3},{3,4},{4,5},{5,6},{6,7},{7,8},{8,9},{9,10},{10,1... | collective-permute-start | bytes 4718600 | tf_op jit(solution)/shard_map/ppermute | solution.py:20
  23.0 1.9 %collective-permute-start.1 = (bf16[2,12,128,256]{3,2,1,0:T(8,128)(2,1)}, bf16[2,12,128,256]{3,2,1,0:T(8,128)(2,1)}, u32[]{:S(2)}, u32[]{:S(2)}) collective-permute-start(bf16[2,12,128,256]{3,2,1,0:T(8,128)(2,1)} %get-tuple-element.14), channel_id=1, source_target_pairs={{1,0},{2,1},{3,2},{4,3},{5,4},{6,5},{7,6},{8,7},{9,8},{10,9},{11,1... | collective-permute-start | bytes 4718600 | tf_op jit(solution)/shard_map/ppermute | solution.py:20
  24.9 0.0 copy-done.4
  25.0 0.0 copy-done.6
  25.0 0.0 copy-done.1
  25.0 0.0 copy-done.2
  25.0 12.5 %operators.1 = (bf16[4,384,384]{2,1,0:T(8,128)(2,1)S(1)}, bf16[4,384,384]{2,1,0:T(8,128)(2,1)}) custom-call(s32[48,384]{1,0:T(8,128)S(1)} %bitcast.9, s32[48,384]{1,0:T(8,128)S(1)} %bitcast.10, s32[1,384]{1,0:T(1,128)S(1)} %broadcast_in_dim.3.count_ref, f32[8,384]{1,0:T(8,128)S(1)} %pad.4.table_ref), custom_call_target="tpu_custom_call" | custom-call | flops 12000000000 | bytes 3000000 | tf_op jit(solution)/shard_map/operators/pallas_call | solution.py:238
  37.5 6.5 %all-to-all-done = bf16[128,8,768]{2,1,0:T(8,128)(2,1)S(1)} async-done(((bf16[128,8,768]{2,1,0:T(8,128)(2,1)}), bf16[128,8,768]{2,1,0:T(8,128)(2,1)S(1)}, u32[]{:S(2)}, u32[]{:S(2)}) %all-to-all-start) | async-done | bytes 1572896 | tf_op jit(solution)/shard_map/all_to_all | solution.py:476
  44.0 4.8 %translate.1 = bf16[1024,768]{1,0:T(8,128)(2,1)} custom-call(bf16[1024,768]{1,0:T(8,128)(2,1)S(1)} %bitcast.7, bf16[4,384,384]{2,1,0:T(8,128)(2,1)S(1)} %get-tuple-element.11.m_ref, bf16[4,384,384]{2,1,0:T(8,128)(2,1)} %get-tuple-element.12.rest_hbm), custom_call_target="tpu_custom_call" | custom-call | flops 1200000000 | bytes 5500000 | tf_op jit(solution)/shard_map/translate/pallas_call | solution.py:300
  48.9 0.0 copy-start.5
  48.9 5.0 %all-to-all-start.1 = ((bf16[128,8,768]{2,1,0:T(8,128)(2,1)}), bf16[128,8,768]{2,1,0:T(8,128)(2,1)S(1)}, u32[]{:S(2)}, u32[]{:S(2)}) async-start(bf16[128,8,768]{2,1,0:T(8,128)(2,1)} %bitcast.5), calls=%async_computation.1 | async-start | bytes 3145728 | tf_op jit(solution)/shard_map/all_to_all | solution.py:476
  53.9 0.0 copy-done.5
  53.9 0.1 copy.15
  54.0 0.7 reshape.11.index_ref
  54.6 0.0 copy-start
  54.6 0.0 copy-start.3
  54.6 0.0 collective-permute-done.low_ref
  54.7 0.3 collective-permute-done.1.up_ref
  54.9 17.1 %near.1.near_hbm = bf16[24,256,256]{2,1,0:T(8,128)(2,1)} custom-call(s32[216]{0:T(256)} %reshape.11.index_ref, s32[24]{0:T(128)} %count_ref.1, bf16[2,12,128,256]{3,2,1,0:T(8,128)(2,1)} %collective-permute-done.low_ref, bf16[2,24,128,256]{3,2,1,0:T(8,128)(2,1)} %cur_ref.1, bf16[2,12,128,256]{3,2,1,0:T(8,128)(2,1)} %collective-permute-done.1.up_ref, ...), custom_call_target="tpu_custom_call" | custom-call | flops 7200000000 | bytes 27000000 | tf_op jit(solution)/shard_map/near/pallas_call | solution.py:359
  72.0 6.5 %all-to-all-done.1 = bf16[128,8,768]{2,1,0:T(8,128)(2,1)S(1)} async-done(((bf16[128,8,768]{2,1,0:T(8,128)(2,1)}), bf16[128,8,768]{2,1,0:T(8,128)(2,1)S(1)}, u32[]{:S(2)}, u32[]{:S(2)}) %all-to-all-start.1) | async-done | bytes 1572896 | tf_op jit(solution)/shard_map/all_to_all | solution.py:476
  78.5 0.0 copy-done
  78.5 0.0 copy-done.3
  78.5 6.2 %downward.1 = bf16[2,24,128,256]{3,2,1,0:T(8,128)(2,1)} custom-call(bf16[1024,768]{1,0:T(8,128)(2,1)S(1)} %bitcast.8, bf16[512,128]{1,0:T(8,128)(2,1)S(1)} %copy-done, f32[8,512]{1,0:T(8,128)S(1)} %copy-done.3, bf16[24,2,128,128]{3,2,1,0:T(8,128)(2,1)} %rec_hbm.1, bf16[24,256,256]{2,1,0:T(8,128)(2,1)} %near.1.near_hbm), custom_call_target="tpu_custom_call" | custom-call | flops 5000000000 | bytes 13000000 | tf_op jit(solution)/shard_map/downward/pallas_call | solution.py:448
  (5 shorter events, 0.0 us)
Async XLA Ops:
  7.9 17.0 %copy-start.4 = (f32[316,2,4]{0,2,1:T(4,128)S(1)}, f32[316,2,4]{0,2,1:T(4,128)}, u32[]{:S(2)}) copy-start(f32[316,2,4]{0,2,1:T(4,128)} %param.23) | copy-start | bytes 30340
  7.9 17.1 %copy-start.6 = (s32[384]{0:T(512)S(1)}, s32[384]{0:T(512)}, u32[]{:S(2)}) copy-start(s32[384]{0:T(512)} %param.21) | copy-start | bytes 4612
  7.9 17.1 %copy-start.1 = (s32[384,48]{0,1:T(8,128)S(1)}, s32[384,48]{0,1:T(8,128)}, u32[]{:S(2)}) copy-start(s32[384,48]{0,1:T(8,128)} %param.20) | copy-start | bytes 221188
  7.9 17.1 %copy-start.2 = (s32[384,48]{0,1:T(8,128)S(1)}, s32[384,48]{0,1:T(8,128)}, u32[]{:S(2)}) copy-start(s32[384,48]{0,1:T(8,128)} %param.22) | copy-start | bytes 221188
  7.9 36.1 %all-to-all-start = ((bf16[128,8,768]{2,1,0:T(8,128)(2,1)}), bf16[128,8,768]{2,1,0:T(8,128)(2,1)S(1)}, u32[]{:S(2)}, u32[]{:S(2)}) async-start(bf16[128,8,768]{2,1,0:T(8,128)(2,1)} %bitcast.11), calls=%async_computation | async-start | bytes 3145728 | tf_op jit(solution)/shard_map/all_to_all | solution.py:476
  19.4 35.2 %collective-permute-start = (bf16[2,12,128,256]{3,2,1,0:T(8,128)(2,1)}, bf16[2,12,128,256]{3,2,1,0:T(8,128)(2,1)}, u32[]{:S(2)}, u32[]{:S(2)}) collective-permute-start(bf16[2,12,128,256]{3,2,1,0:T(8,128)(2,1)} %get-tuple-element.13), channel_id=1, source_target_pairs={{0,1},{1,2},{2,3},{3,4},{4,5},{5,6},{6,7},{7,8},{8,9},{9,10},{10,1... | collective-permute-start | bytes 4718600 | tf_op jit(solution)/shard_map/ppermute | solution.py:20
  23.0 31.9 %collective-permute-start.1 = (bf16[2,12,128,256]{3,2,1,0:T(8,128)(2,1)}, bf16[2,12,128,256]{3,2,1,0:T(8,128)(2,1)}, u32[]{:S(2)}, u32[]{:S(2)}) collective-permute-start(bf16[2,12,128,256]{3,2,1,0:T(8,128)(2,1)} %get-tuple-element.14), channel_id=1, source_target_pairs={{1,0},{2,1},{3,2},{4,3},{5,4},{6,5},{7,6},{8,7},{9,8},{10,9},{11,1... | collective-permute-start | bytes 4718600 | tf_op jit(solution)/shard_map/ppermute | solution.py:20
  48.9 5.0 %copy-start.5 = (s32[24,9]{0,1:T(8,128)S(1)}, s32[24,9]{0,1:T(8,128)}, u32[]{:S(2)}) copy-start(s32[24,9]{0,1:T(8,128)} %param.14) | copy-start | bytes 2596
  48.9 29.7 %all-to-all-start.1 = ((bf16[128,8,768]{2,1,0:T(8,128)(2,1)}), bf16[128,8,768]{2,1,0:T(8,128)(2,1)S(1)}, u32[]{:S(2)}, u32[]{:S(2)}) async-start(bf16[128,8,768]{2,1,0:T(8,128)(2,1)} %bitcast.5), calls=%async_computation.1 | async-start | bytes 3145728 | tf_op jit(solution)/shard_map/all_to_all | solution.py:476
  54.6 23.9 %copy-start = (bf16[512,128]{1,0:T(8,128)(2,1)S(1)}, bf16[512,128]{1,0:T(8,128)(2,1)}, u32[]{:S(2)}) copy-start(bf16[512,128]{1,0:T(8,128)(2,1)} %interp_ref.3) | copy-start | bytes 393220
  54.6 23.9 %copy-start.3 = (f32[8,512]{1,0:T(8,128)S(1)}, f32[8,512]{1,0:T(8,128)}, u32[]{:S(2)}) copy-start(f32[8,512]{1,0:T(8,128)} %angle_ref.3) | copy-start | bytes 49156

commit v3 on v2

--- a/solution.py
+++ b/solution.py
@@ -256,7 +256,7 @@
     )(far, trans, count, table)
 
 
-def translate_kernel(x_ref, m_ref, rest_hbm, out_ref, rest_ref, xp_ref, yp_ref, sem):
+def translate_kernel(x_ref, m_ref, rest_hbm, out_hbm, rest_ref, xp_ref, yp_ref, out_ref, sem, out_sems):
     groups = 4
     rows = x_ref.shape[0] // groups
     share = rows // 8
@@ -291,8 +291,14 @@
                     yp_ref[
                         g, (c * 4 + j) * share : (c * 4 + j + 1) * share, p * 256 : (p + 1) * 256
                     ] = y[start : start + share]
+    going = []
     for g in range(groups):
         out_ref[g * rows : (g + 1) * rows, :] = dot(scatter, yp_ref[g]).astype(BF16)
+        of = pl.ds(g * rows, rows)
+        going.append(pltpu.make_async_copy(out_ref.at[of], out_hbm.at[of], out_sems.at[g]))
+        going[-1].start()
+    for copy in going:
+        copy.wait()
 
 
 def translate(x, matrix, rest):
@@ -301,13 +307,15 @@
         translate_kernel,
         in_specs=[pl.BlockSpec(memory_space=pltpu.VMEM)] * 2
         + [pl.BlockSpec(memory_space=pltpu.HBM)],
-        out_specs=pl.BlockSpec(memory_space=pltpu.VMEM),
-        out_shape=jax.ShapeDtypeStruct(x.shape, BF16),
+        out_specs=pl.BlockSpec(memory_space=pltpu.HBM),
+        out_shape=pltpu.HBM(x.shape, BF16),
         scratch_shapes=[
             pltpu.VMEM(rest.shape, BF16),
             pltpu.VMEM((4, rows // 4, width), BF16),
             pltpu.VMEM((4, rows // 4, width), BF16),
+            pltpu.VMEM(x.shape, BF16),
             pltpu.SemaphoreType.DMA((1,)),
+            pltpu.SemaphoreType.DMA((4,)),
         ],
         compiler_params=pltpu.CompilerParams(vmem_limit_bytes=32 * MIB),
         cost_estimate=pl.CostEstimate(flops=1_200_000_000, bytes_accessed=5_500_000, transcendentals=0),

time: 85.6 us -> 85.3 us (level)
  transfers between devices with their start and end apart: 4 -> 4, of which waited for: 3 -> 3; matrix products, arithmetic and copies ran while one was open for 1% -> 1% of each run, Pallas kernels for 41% -> 40%
where the time goes in v3:
time: 85.3 us; the launch traced here: 84.6 us
  Pallas kernels  47.8 us (56%)
  starting transfers between devices  22 us (26%)
  waiting for transfers between devices  13.7 us (16%)
    pallas_call x1, Pallas kernels, near(): pl.pallas_call(near_kernel, grid_spec=pltpu.PrefetchScalarGridSpec(num_sc...  16.7 us
    all_to_all x2, starting transfers between devices, exchanged(): return lax.all_to_all(value, AXES, split_axis=0, concat_axis=0, tiled=True)  16.5 us
    all_to_all x2, waiting for transfers between devices, exchanged(): return lax.all_to_all(value, AXES, split_axis=0, concat_axis=0, tiled=True)  13.1 us
    pallas_call x1, Pallas kernels, operators(): pl.pallas_call(operators_kernel, in_specs=[pl.BlockSpec(memory_space=pltp...  12.5 us
    pallas_call x1, Pallas kernels, upward(): pl.pallas_call(upward_kernel, in_specs=[pl.BlockSpec(memory_space=pltpu.H...  7.88 us
    pallas_call x1, Pallas kernels, downward(): pl.pallas_call(downward_kernel, in_specs=[pl.BlockSpec(memory_space=pltpu...  6.22 us
    ppermute x2, starting transfers between devices, passed_along(): return lax.ppermute(value, axis, pairs)  5.47 us
    pallas_call x1, Pallas kernels, translate(): pl.pallas_call(translate_kernel, in_specs=[pl.BlockSpec(memory_space=pltp...  4.55 us
  transfers between devices with their start and end apart: 4, of which 3 were waited for; matrix products, arithmetic and copies ran while one was open for 1% of the time, Pallas kernels for 40%

profile of v3, /device:TPU:1, one launch (start us, length us, event | category | flops | bytes accessed | tf_op | source)
XLA Modules:
  0.0 84.6 jit_solution(15578691668012587070)
XLA Ops:
  0.0 7.9 %upward.1 = (bf16[1024,768]{1,0:T(8,128)(2,1)}, bf16[2,12,128,256]{3,2,1,0:T(8,128)(2,1)}, bf16[2,12,128,256]{3,2,1,0:T(8,128)(2,1)}) custom-call(bf16[2,24,128,256]{3,2,1,0:T(8,128)(2,1)} %cur_ref.1, bf16[24,2,128,128]{3,2,1,0:T(8,128)(2,1)} %rad_hbm.1, bf16[512,128]{1,0:T(8,128)(2,1)} %interp_ref.3, f32[8,512]{1,0:T(8,128)} %angle_ref.3), custom_call_target="tpu_custom_call" | custom-call | flops 5000000000 | bytes 7000000 | tf_op jit(solution)/shard_map/upward/pallas_call | solution.py:149
  7.9 0.0 copy-start.4
  7.9 0.0 copy-start.6
  7.9 0.0 copy-start.1
  7.9 0.0 copy-start.2
  7.9 11.5 %all-to-all-start = ((bf16[128,8,768]{2,1,0:T(8,128)(2,1)}), bf16[128,8,768]{2,1,0:T(8,128)(2,1)S(1)}, u32[]{:S(2)}, u32[]{:S(2)}) async-start(bf16[128,8,768]{2,1,0:T(8,128)(2,1)} %bitcast.12), calls=%async_computation | async-start | bytes 3145728 | tf_op jit(solution)/shard_map/all_to_all | solution.py:484
  19.4 3.5 %collective-permute-start = (bf16[2,12,128,256]{3,2,1,0:T(8,128)(2,1)}, bf16[2,12,128,256]{3,2,1,0:T(8,128)(2,1)}, u32[]{:S(2)}, u32[]{:S(2)}) collective-permute-start(bf16[2,12,128,256]{3,2,1,0:T(8,128)(2,1)} %get-tuple-element.13), channel_id=1, source_target_pairs={{0,1},{1,2},{2,3},{3,4},{4,5},{5,6},{6,7},{7,8},{8,9},{9,10},{10,1... | collective-permute-start | bytes 4718600 | tf_op jit(solution)/shard_map/ppermute | solution.py:20
  23.0 1.9 %collective-permute-start.1 = (bf16[2,12,128,256]{3,2,1,0:T(8,128)(2,1)}, bf16[2,12,128,256]{3,2,1,0:T(8,128)(2,1)}, u32[]{:S(2)}, u32[]{:S(2)}) collective-permute-start(bf16[2,12,128,256]{3,2,1,0:T(8,128)(2,1)} %get-tuple-element.14), channel_id=1, source_target_pairs={{1,0},{2,1},{3,2},{4,3},{5,4},{6,5},{7,6},{8,7},{9,8},{10,9},{11,1... | collective-permute-start | bytes 4718600 | tf_op jit(solution)/shard_map/ppermute | solution.py:20
  24.9 0.0 copy-done.4
  25.0 0.0 copy-done.6
  25.0 0.0 copy-done.1
  25.0 0.0 copy-done.2
  25.0 12.5 %operators.1 = (bf16[4,384,384]{2,1,0:T(8,128)(2,1)S(1)}, bf16[4,384,384]{2,1,0:T(8,128)(2,1)}) custom-call(s32[48,384]{1,0:T(8,128)S(1)} %bitcast.9, s32[48,384]{1,0:T(8,128)S(1)} %bitcast.10, s32[1,384]{1,0:T(1,128)S(1)} %broadcast_in_dim.3.count_ref, f32[8,384]{1,0:T(8,128)S(1)} %pad.4.table_ref), custom_call_target="tpu_custom_call" | custom-call | flops 12000000000 | bytes 3000000 | tf_op jit(solution)/shard_map/operators/pallas_call | solution.py:238
  37.5 6.5 %all-to-all-done = bf16[128,8,768]{2,1,0:T(8,128)(2,1)S(1)} async-done(((bf16[128,8,768]{2,1,0:T(8,128)(2,1)}), bf16[128,8,768]{2,1,0:T(8,128)(2,1)S(1)}, u32[]{:S(2)}, u32[]{:S(2)}) %all-to-all-start) | async-done | bytes 1572896 | tf_op jit(solution)/shard_map/all_to_all | solution.py:484
  44.0 4.6 %translate.1 = bf16[1024,768]{1,0:T(8,128)(2,1)} custom-call(bf16[1024,768]{1,0:T(8,128)(2,1)S(1)} %bitcast.7, bf16[4,384,384]{2,1,0:T(8,128)(2,1)S(1)} %get-tuple-element.11.m_ref, bf16[4,384,384]{2,1,0:T(8,128)(2,1)} %get-tuple-element.12.rest_hbm), custom_call_target="tpu_custom_call" | custom-call | flops 1200000000 | bytes 5500000 | tf_op jit(solution)/shard_map/translate/pallas_call | solution.py:306
  48.6 0.0 copy-start.5
  48.6 5.0 %all-to-all-start.1 = ((bf16[128,8,768]{2,1,0:T(8,128)(2,1)}), bf16[128,8,768]{2,1,0:T(8,128)(2,1)S(1)}, u32[]{:S(2)}, u32[]{:S(2)}) async-start(bf16[128,8,768]{2,1,0:T(8,128)(2,1)} %bitcast.11), calls=%async_computation.1 | async-start | bytes 3145728 | tf_op jit(solution)/shard_map/all_to_all | solution.py:484
  53.6 0.0 copy-done.5
  53.6 0.1 copy.15
  53.7 0.7 reshape.11.index_ref
  54.4 0.0 copy-start
  54.4 0.0 copy-start.3
  54.4 0.0 collective-permute-done.low_ref
  54.4 0.6 collective-permute-done.1.up_ref
  54.9 16.7 %near.1.near_hbm = bf16[24,256,256]{2,1,0:T(8,128)(2,1)} custom-call(s32[216]{0:T(256)} %reshape.11.index_ref, s32[24]{0:T(128)} %count_ref.1, bf16[2,12,128,256]{3,2,1,0:T(8,128)(2,1)} %collective-permute-done.low_ref, bf16[2,24,128,256]{3,2,1,0:T(8,128)(2,1)} %cur_ref.1, bf16[2,12,128,256]{3,2,1,0:T(8,128)(2,1)} %collective-permute-done.1.up_ref, ...), custom_call_target="tpu_custom_call" | custom-call | flops 7200000000 | bytes 27000000 | tf_op jit(solution)/shard_map/near/pallas_call | solution.py:367
  71.7 6.6 %all-to-all-done.1 = bf16[128,8,768]{2,1,0:T(8,128)(2,1)S(1)} async-done(((bf16[128,8,768]{2,1,0:T(8,128)(2,1)}), bf16[128,8,768]{2,1,0:T(8,128)(2,1)S(1)}, u32[]{:S(2)}, u32[]{:S(2)}) %all-to-all-start.1) | async-done | bytes 1572896 | tf_op jit(solution)/shard_map/all_to_all | solution.py:484
  78.2 0.0 copy-done
  78.2 0.0 copy-done.3
  78.3 6.2 %downward.1 = bf16[2,24,128,256]{3,2,1,0:T(8,128)(2,1)} custom-call(bf16[1024,768]{1,0:T(8,128)(2,1)S(1)} %bitcast.8, bf16[512,128]{1,0:T(8,128)(2,1)S(1)} %copy-done, f32[8,512]{1,0:T(8,128)S(1)} %copy-done.3, bf16[24,2,128,128]{3,2,1,0:T(8,128)(2,1)} %rec_hbm.1, bf16[24,256,256]{2,1,0:T(8,128)(2,1)} %near.1.near_hbm), custom_call_target="tpu_custom_call" | custom-call | flops 5000000000 | bytes 13000000 | tf_op jit(solution)/shard_map/downward/pallas_call | solution.py:456
  (5 shorter events, 0.0 us)
Async XLA Ops:
  7.9 17.0 %copy-start.4 = (f32[316,2,4]{0,2,1:T(4,128)S(1)}, f32[316,2,4]{0,2,1:T(4,128)}, u32[]{:S(2)}) copy-start(f32[316,2,4]{0,2,1:T(4,128)} %param.23) | copy-start | bytes 30340
  7.9 17.1 %copy-start.6 = (s32[384]{0:T(512)S(1)}, s32[384]{0:T(512)}, u32[]{:S(2)}) copy-start(s32[384]{0:T(512)} %param.21) | copy-start | bytes 4612
  7.9 17.1 %copy-start.1 = (s32[384,48]{0,1:T(8,128)S(1)}, s32[384,48]{0,1:T(8,128)}, u32[]{:S(2)}) copy-start(s32[384,48]{0,1:T(8,128)} %param.20) | copy-start | bytes 221188
  7.9 17.1 %copy-start.2 = (s32[384,48]{0,1:T(8,128)S(1)}, s32[384,48]{0,1:T(8,128)}, u32[]{:S(2)}) copy-start(s32[384,48]{0,1:T(8,128)} %param.22) | copy-start | bytes 221188
  7.9 36.1 %all-to-all-start = ((bf16[128,8,768]{2,1,0:T(8,128)(2,1)}), bf16[128,8,768]{2,1,0:T(8,128)(2,1)S(1)}, u32[]{:S(2)}, u32[]{:S(2)}) async-start(bf16[128,8,768]{2,1,0:T(8,128)(2,1)} %bitcast.12), calls=%async_computation | async-start | bytes 3145728 | tf_op jit(solution)/shard_map/all_to_all | solution.py:484
  19.4 34.9 %collective-permute-start = (bf16[2,12,128,256]{3,2,1,0:T(8,128)(2,1)}, bf16[2,12,128,256]{3,2,1,0:T(8,128)(2,1)}, u32[]{:S(2)}, u32[]{:S(2)}) collective-permute-start(bf16[2,12,128,256]{3,2,1,0:T(8,128)(2,1)} %get-tuple-element.13), channel_id=1, source_target_pairs={{0,1},{1,2},{2,3},{3,4},{4,5},{5,6},{6,7},{7,8},{8,9},{9,10},{10,1... | collective-permute-start | bytes 4718600 | tf_op jit(solution)/shard_map/ppermute | solution.py:20
  23.0 31.9 %collective-permute-start.1 = (bf16[2,12,128,256]{3,2,1,0:T(8,128)(2,1)}, bf16[2,12,128,256]{3,2,1,0:T(8,128)(2,1)}, u32[]{:S(2)}, u32[]{:S(2)}) collective-permute-start(bf16[2,12,128,256]{3,2,1,0:T(8,128)(2,1)} %get-tuple-element.14), channel_id=1, source_target_pairs={{1,0},{2,1},{3,2},{4,3},{5,4},{6,5},{7,6},{8,7},{9,8},{10,9},{11,1... | collective-permute-start | bytes 4718600 | tf_op jit(solution)/shard_map/ppermute | solution.py:20
  48.6 5.0 %copy-start.5 = (s32[24,9]{0,1:T(8,128)S(1)}, s32[24,9]{0,1:T(8,128)}, u32[]{:S(2)}) copy-start(s32[24,9]{0,1:T(8,128)} %param.14) | copy-start | bytes 2596
  48.6 29.7 %all-to-all-start.1 = ((bf16[128,8,768]{2,1,0:T(8,128)(2,1)}), bf16[128,8,768]{2,1,0:T(8,128)(2,1)S(1)}, u32[]{:S(2)}, u32[]{:S(2)}) async-start(bf16[128,8,768]{2,1,0:T(8,128)(2,1)} %bitcast.11), calls=%async_computation.1 | async-start | bytes 3145728 | tf_op jit(solution)/shard_map/all_to_all | solution.py:484
  54.4 23.9 %copy-start = (bf16[512,128]{1,0:T(8,128)(2,1)S(1)}, bf16[512,128]{1,0:T(8,128)(2,1)}, u32[]{:S(2)}) copy-start(bf16[512,128]{1,0:T(8,128)(2,1)} %interp_ref.3) | copy-start | bytes 393220
  54.4 23.9 %copy-start.3 = (f32[8,512]{1,0:T(8,128)S(1)}, f32[8,512]{1,0:T(8,128)}, u32[]{:S(2)}) copy-start(f32[8,512]{1,0:T(8,128)} %angle_ref.3) | copy-start | bytes 49156

commit v4 on v3

--- a/solution.py
+++ b/solution.py
@@ -162,9 +162,9 @@
             pltpu.VMEM((2 * directions, 2048), BF16),
             pltpu.VMEM((2048, 256), BF16),
             pltpu.VMEM((parents, 2 * directions, columns), BF16),
-            pltpu.SemaphoreType.DMA((parents, 2)),
+            pltpu.SemaphoreType.DMA((parents, 4)),
             pltpu.SemaphoreType.DMA((2,)),
-            pltpu.SemaphoreType.DMA((parents, 2)),
+            pltpu.SemaphoreType.DMA((parents, 4)),
         ],
         compiler_params=pltpu.CompilerParams(vmem_limit_bytes=60 * MIB),
         cost_estimate=pl.CostEstimate(flops=5_000_000_000, bytes_accessed=7_000_000, transcendentals=0),
@@ -226,7 +226,7 @@
         rest_ref[:, rows, :] = matrix[4:]
         return carry
 
-    lax.fori_loop(0, blocks, body, 0, unroll=2)
+    lax.fori_loop(0, blocks, body, 0, unroll=4)
     copy = pltpu.make_async_copy(rest_ref, rest_hbm, sem.at[0])
     copy.start()
     copy.wait()

time: 85.3 us -> 85.3 us (level)
  waiting for transfers between devices: 13.7 us -> 15.4 us
  Pallas kernels: 47.8 us -> 46.1 us
    all_to_all x2, waiting for transfers between devices: 13.1 us -> 14.8 us  [exchanged(): return lax.all_to_all(value, AXES, split_axis=0, concat_axis=0, tiled=True)]
    pallas_call x1, Pallas kernels: 12.5 us -> 11.2 us  [operators(): pl.pallas_call(operators_kernel, in_specs=[pl.BlockSpec(memory_space=pltp...]
  transfers between devices with their start and end apart: 4 -> 4, of which waited for: 3 -> 3; matrix products, arithmetic and copies ran while one was open for 1% -> 1% of each run, Pallas kernels for 40% -> 38%
where the time goes in v4:
time: 85.3 us; the launch traced here: 84.7 us
  Pallas kernels  46.1 us (54%)
  starting transfers between devices  22 us (26%)
  waiting for transfers between devices  15.4 us (18%)
    all_to_all x2, starting transfers between devices, exchanged(): return lax.all_to_all(value, AXES, split_axis=0, concat_axis=0, tiled=True)  16.5 us
    pallas_call x1, Pallas kernels, near(): pl.pallas_call(near_kernel, grid_spec=pltpu.PrefetchScalarGridSpec(num_sc...  16.3 us
    all_to_all x2, waiting for transfers between devices, exchanged(): return lax.all_to_all(value, AXES, split_axis=0, concat_axis=0, tiled=True)  14.8 us
    pallas_call x1, Pallas kernels, operators(): pl.pallas_call(operators_kernel, in_specs=[pl.BlockSpec(memory_space=pltp...  11.2 us
    pallas_call x1, Pallas kernels, upward(): pl.pallas_call(upward_kernel, in_specs=[pl.BlockSpec(memory_space=pltpu.H...  7.9 us
    pallas_call x1, Pallas kernels, downward(): pl.pallas_call(downward_kernel, in_specs=[pl.BlockSpec(memory_space=pltpu...  6.22 us
    ppermute x2, starting transfers between devices, passed_along(): return lax.ppermute(value, axis, pairs)  5.47 us
    pallas_call x1, Pallas kernels, translate(): pl.pallas_call(translate_kernel, in_specs=[pl.BlockSpec(memory_space=pltp...  4.55 us
  transfers between devices with their start and end apart: 4, of which 3 were waited for; matrix products, arithmetic and copies ran while one was open for 1% of the time, Pallas kernels for 38%

profile of v4, /device:TPU:1, one launch (start us, length us, event | category | flops | bytes accessed | tf_op | source)
XLA Modules:
  0.0 84.7 jit_solution(10591875063393689022)
XLA Ops:
  0.0 7.9 %upward.1 = (bf16[1024,768]{1,0:T(8,128)(2,1)}, bf16[2,12,128,256]{3,2,1,0:T(8,128)(2,1)}, bf16[2,12,128,256]{3,2,1,0:T(8,128)(2,1)}) custom-call(bf16[2,24,128,256]{3,2,1,0:T(8,128)(2,1)} %cur_ref.1, bf16[24,2,128,128]{3,2,1,0:T(8,128)(2,1)} %rad_hbm.1, bf16[512,128]{1,0:T(8,128)(2,1)} %interp_ref.3, f32[8,512]{1,0:T(8,128)} %angle_ref.3), custom_call_target="tpu_custom_call" | custom-call | flops 5000000000 | bytes 7000000 | tf_op jit(solution)/shard_map/upward/pallas_call | solution.py:149
  7.9 0.0 copy-start.4
  7.9 0.0 copy-start.6
  7.9 0.0 copy-start.1
  7.9 0.0 copy-start.2
  8.0 11.5 %all-to-all-start = ((bf16[128,8,768]{2,1,0:T(8,128)(2,1)}), bf16[128,8,768]{2,1,0:T(8,128)(2,1)S(1)}, u32[]{:S(2)}, u32[]{:S(2)}) async-start(bf16[128,8,768]{2,1,0:T(8,128)(2,1)} %bitcast.12), calls=%async_computation | async-start | bytes 3145728 | tf_op jit(solution)/shard_map/all_to_all | solution.py:484
  19.5 3.5 %collective-permute-start = (bf16[2,12,128,256]{3,2,1,0:T(8,128)(2,1)}, bf16[2,12,128,256]{3,2,1,0:T(8,128)(2,1)}, u32[]{:S(2)}, u32[]{:S(2)}) collective-permute-start(bf16[2,12,128,256]{3,2,1,0:T(8,128)(2,1)} %get-tuple-element.13), channel_id=1, source_target_pairs={{0,1},{1,2},{2,3},{3,4},{4,5},{5,6},{6,7},{7,8},{8,9},{9,10},{10,1... | collective-permute-start | bytes 4718600 | tf_op jit(solution)/shard_map/ppermute | solution.py:20
  23.0 1.9 %collective-permute-start.1 = (bf16[2,12,128,256]{3,2,1,0:T(8,128)(2,1)}, bf16[2,12,128,256]{3,2,1,0:T(8,128)(2,1)}, u32[]{:S(2)}, u32[]{:S(2)}) collective-permute-start(bf16[2,12,128,256]{3,2,1,0:T(8,128)(2,1)} %get-tuple-element.14), channel_id=1, source_target_pairs={{1,0},{2,1},{3,2},{4,3},{5,4},{6,5},{7,6},{8,7},{9,8},{10,9},{11,1... | collective-permute-start | bytes 4718600 | tf_op jit(solution)/shard_map/ppermute | solution.py:20
  24.9 0.0 copy-done.4
  25.0 0.0 copy-done.6
  25.0 0.0 copy-done.1
  25.0 0.0 copy-done.2
  25.0 11.2 %operators.1 = (bf16[4,384,384]{2,1,0:T(8,128)(2,1)S(1)}, bf16[4,384,384]{2,1,0:T(8,128)(2,1)}) custom-call(s32[48,384]{1,0:T(8,128)S(1)} %bitcast.9, s32[48,384]{1,0:T(8,128)S(1)} %bitcast.10, s32[1,384]{1,0:T(1,128)S(1)} %broadcast_in_dim.3.count_ref, f32[8,384]{1,0:T(8,128)S(1)} %pad.4.table_ref), custom_call_target="tpu_custom_call" | custom-call | flops 12000000000 | bytes 3000000 | tf_op jit(solution)/shard_map/operators/pallas_call | solution.py:238
  36.2 7.8 %all-to-all-done = bf16[128,8,768]{2,1,0:T(8,128)(2,1)S(1)} async-done(((bf16[128,8,768]{2,1,0:T(8,128)(2,1)}), bf16[128,8,768]{2,1,0:T(8,128)(2,1)S(1)}, u32[]{:S(2)}, u32[]{:S(2)}) %all-to-all-start) | async-done | bytes 1572896 | tf_op jit(solution)/shard_map/all_to_all | solution.py:484
  44.0 4.6 %translate.1 = bf16[1024,768]{1,0:T(8,128)(2,1)} custom-call(bf16[1024,768]{1,0:T(8,128)(2,1)S(1)} %bitcast.7, bf16[4,384,384]{2,1,0:T(8,128)(2,1)S(1)} %get-tuple-element.11.m_ref, bf16[4,384,384]{2,1,0:T(8,128)(2,1)} %get-tuple-element.12.rest_hbm), custom_call_target="tpu_custom_call" | custom-call | flops 1200000000 | bytes 5500000 | tf_op jit(solution)/shard_map/translate/pallas_call | solution.py:306
  48.6 0.0 copy-start.5
  48.6 5.0 %all-to-all-start.1 = ((bf16[128,8,768]{2,1,0:T(8,128)(2,1)}), bf16[128,8,768]{2,1,0:T(8,128)(2,1)S(1)}, u32[]{:S(2)}, u32[]{:S(2)}) async-start(bf16[128,8,768]{2,1,0:T(8,128)(2,1)} %bitcast.11), calls=%async_computation.1 | async-start | bytes 3145728 | tf_op jit(solution)/shard_map/all_to_all | solution.py:484
  53.6 0.0 copy-done.5
  53.6 0.1 copy.15
  53.7 0.7 reshape.11.index_ref
  54.4 0.0 copy-start
  54.4 0.0 copy-start.3
  54.4 0.0 collective-permute-done.low_ref
  54.4 0.6 collective-permute-done.1.up_ref
  55.0 16.3 %near.1.near_hbm = bf16[24,256,256]{2,1,0:T(8,128)(2,1)} custom-call(s32[216]{0:T(256)} %reshape.11.index_ref, s32[24]{0:T(128)} %count_ref.1, bf16[2,12,128,256]{3,2,1,0:T(8,128)(2,1)} %collective-permute-done.low_ref, bf16[2,24,128,256]{3,2,1,0:T(8,128)(2,1)} %cur_ref.1, bf16[2,12,128,256]{3,2,1,0:T(8,128)(2,1)} %collective-permute-done.1.up_ref, ...), custom_call_target="tpu_custom_call" | custom-call | flops 7200000000 | bytes 27000000 | tf_op jit(solution)/shard_map/near/pallas_call | solution.py:367
  71.3 7.0 %all-to-all-done.1 = bf16[128,8,768]{2,1,0:T(8,128)(2,1)S(1)} async-done(((bf16[128,8,768]{2,1,0:T(8,128)(2,1)}), bf16[128,8,768]{2,1,0:T(8,128)(2,1)S(1)}, u32[]{:S(2)}, u32[]{:S(2)}) %all-to-all-start.1) | async-done | bytes 1572896 | tf_op jit(solution)/shard_map/all_to_all | solution.py:484
  78.3 0.0 copy-done
  78.3 0.0 copy-done.3
  78.3 6.2 %downward.1 = bf16[2,24,128,256]{3,2,1,0:T(8,128)(2,1)} custom-call(bf16[1024,768]{1,0:T(8,128)(2,1)S(1)} %bitcast.8, bf16[512,128]{1,0:T(8,128)(2,1)S(1)} %copy-done, f32[8,512]{1,0:T(8,128)S(1)} %copy-done.3, bf16[24,2,128,128]{3,2,1,0:T(8,128)(2,1)} %rec_hbm.1, bf16[24,256,256]{2,1,0:T(8,128)(2,1)} %near.1.near_hbm), custom_call_target="tpu_custom_call" | custom-call | flops 5000000000 | bytes 13000000 | tf_op jit(solution)/shard_map/downward/pallas_call | solution.py:456
  (5 shorter events, 0.0 us)
Async XLA Ops:
  7.9 17.0 %copy-start.4 = (f32[316,2,4]{0,2,1:T(4,128)S(1)}, f32[316,2,4]{0,2,1:T(4,128)}, u32[]{:S(2)}) copy-start(f32[316,2,4]{0,2,1:T(4,128)} %param.23) | copy-start | bytes 30340
  7.9 17.1 %copy-start.6 = (s32[384]{0:T(512)S(1)}, s32[384]{0:T(512)}, u32[]{:S(2)}) copy-start(s32[384]{0:T(512)} %param.21) | copy-start | bytes 4612
  7.9 17.1 %copy-start.1 = (s32[384,48]{0,1:T(8,128)S(1)}, s32[384,48]{0,1:T(8,128)}, u32[]{:S(2)}) copy-start(s32[384,48]{0,1:T(8,128)} %param.20) | copy-start | bytes 221188
  7.9 17.1 %copy-start.2 = (s32[384,48]{0,1:T(8,128)S(1)}, s32[384,48]{0,1:T(8,128)}, u32[]{:S(2)}) copy-start(s32[384,48]{0,1:T(8,128)} %param.22) | copy-start | bytes 221188
  8.0 36.1 %all-to-all-start = ((bf16[128,8,768]{2,1,0:T(8,128)(2,1)}), bf16[128,8,768]{2,1,0:T(8,128)(2,1)S(1)}, u32[]{:S(2)}, u32[]{:S(2)}) async-start(bf16[128,8,768]{2,1,0:T(8,128)(2,1)} %bitcast.12), calls=%async_computation | async-start | bytes 3145728 | tf_op jit(solution)/shard_map/all_to_all | solution.py:484
  19.5 34.9 %collective-permute-start = (bf16[2,12,128,256]{3,2,1,0:T(8,128)(2,1)}, bf16[2,12,128,256]{3,2,1,0:T(8,128)(2,1)}, u32[]{:S(2)}, u32[]{:S(2)}) collective-permute-start(bf16[2,12,128,256]{3,2,1,0:T(8,128)(2,1)} %get-tuple-element.13), channel_id=1, source_target_pairs={{0,1},{1,2},{2,3},{3,4},{4,5},{5,6},{6,7},{7,8},{8,9},{9,10},{10,1... | collective-permute-start | bytes 4718600 | tf_op jit(solution)/shard_map/ppermute | solution.py:20
  23.0 31.9 %collective-permute-start.1 = (bf16[2,12,128,256]{3,2,1,0:T(8,128)(2,1)}, bf16[2,12,128,256]{3,2,1,0:T(8,128)(2,1)}, u32[]{:S(2)}, u32[]{:S(2)}) collective-permute-start(bf16[2,12,128,256]{3,2,1,0:T(8,128)(2,1)} %get-tuple-element.14), channel_id=1, source_target_pairs={{1,0},{2,1},{3,2},{4,3},{5,4},{6,5},{7,6},{8,7},{9,8},{10,9},{11,1... | collective-permute-start | bytes 4718600 | tf_op jit(solution)/shard_map/ppermute | solution.py:20
  48.6 5.0 %copy-start.5 = (s32[24,9]{0,1:T(8,128)S(1)}, s32[24,9]{0,1:T(8,128)}, u32[]{:S(2)}) copy-start(s32[24,9]{0,1:T(8,128)} %param.14) | copy-start | bytes 2596
  48.6 29.7 %all-to-all-start.1 = ((bf16[128,8,768]{2,1,0:T(8,128)(2,1)}), bf16[128,8,768]{2,1,0:T(8,128)(2,1)S(1)}, u32[]{:S(2)}, u32[]{:S(2)}) async-start(bf16[128,8,768]{2,1,0:T(8,128)(2,1)} %bitcast.11), calls=%async_computation.1 | async-start | bytes 3145728 | tf_op jit(solution)/shard_map/all_to_all | solution.py:484
  54.4 23.9 %copy-start = (bf16[512,128]{1,0:T(8,128)(2,1)S(1)}, bf16[512,128]{1,0:T(8,128)(2,1)}, u32[]{:S(2)}) copy-start(bf16[512,128]{1,0:T(8,128)(2,1)} %interp_ref.3) | copy-start | bytes 393220
  54.4 23.9 %copy-start.3 = (f32[8,512]{1,0:T(8,128)S(1)}, f32[8,512]{1,0:T(8,128)}, u32[]{:S(2)}) copy-start(f32[8,512]{1,0:T(8,128)} %angle_ref.3) | copy-start | bytes 49156
